TPU v7x, 512 devices: a whole 4x4x16 slice. The times are simulated.
512 devices in a mesh: dp: 16 (over y, x_hi, core), blk: 32 (over x_lo, z).
Axes of the slice: x: 4 (x_hi: 2, x_lo: 2; x = x_hi * 2 + x_lo), y: 4, z: 16, core: 2. Of those that a mesh axis runs over, the one named last changes fastest.
Arguments:
- pre_gelu: bfloat16 [98304, 4096], P(('dp', 'blk')), may hold values from -8 to 8
- out_grad: bfloat16 [98304, 1024], P(('dp', 'blk')), may hold values from -6 to 6
- down_weight: bfloat16 [4096, 1024], P('blk'), may hold values from -0.09375 to 0.09375
Outputs:
- block_out: bfloat16 [98304, 1024], P(('dp', 'blk'))
- pre_grad: bfloat16 [98304, 4096], P(('dp', 'blk'))
- weight_grad: float32 [4096, 1024], P('blk')
All inputs are finite; a program needn't handle non-finite values.
Results may differ from a plain program's by a relative error of at most 0.017.
Values may be sent and summed in bfloat16 or wider, within the bound.
A program may use at most 64 MiB of HBM per device.

v0:
```python
import math
import jax
import jax.numpy as jnp
from jax import lax
from jax.sharding import PartitionSpec as P

SQRT_TWO_PI = 0.7978845608028654
CUBIC = 0.044715


def passed_along(array, axis, by):
    peers = lax.axis_size(axis)
    return lax.ppermute(array, axis, [(i, (i + by) % peers) for i in range(peers)])


def gelu_parts(inputs):
    argument = SQRT_TWO_PI * (inputs + CUBIC * inputs * inputs * inputs)
    tangent = jnp.tanh(argument)
    activation = 0.5 * inputs * (1.0 + tangent)
    derivative = 0.5 * (1.0 + tangent) + 0.5 * inputs * (1.0 - tangent * tangent) * SQRT_TWO_PI * (
        1.0 + 3.0 * CUBIC * inputs * inputs
    )
    return (activation, derivative)


def finish_partial(arrived, own_term):
    rounded = (arrived.astype(jnp.float32) + own_term).astype(jnp.bfloat16)
    return lax.optimization_barrier(rounded).astype(jnp.float32)


def body(pre_gelu, out_grad, down_weight):
    row_count = pre_gelu.shape[0]
    model_width = out_grad.shape[1]
    block_rows = down_weight.shape[0]
    cycle_size = lax.axis_size("blk")
    home_index = lax.axis_index("blk")
    activation, derivative = gelu_parts(pre_gelu.astype(jnp.float32))
    hidden = activation.astype(jnp.bfloat16)

    def visit(weight, column, carried):
        out_total, grad_buffer = carried
        part_width = weight.shape[0]
        hidden_part = lax.dynamic_slice_in_dim(hidden, column, part_width, 1)
        slope_part = lax.dynamic_slice_in_dim(derivative, column, part_width, 1)
        out_total = out_total + jnp.dot(hidden_part, weight, preferred_element_type=jnp.float32)
        d_hidden = lax.dot_general(
            out_grad, weight, (((1,), (1,)), ((), ())), preferred_element_type=jnp.float32
        )
        grad_buffer = lax.dynamic_update_slice_in_dim(
            grad_buffer, (d_hidden * slope_part).astype(jnp.bfloat16), column, 1
        )
        contribution = lax.dot_general(
            hidden_part, out_grad, (((0,), (0,)), ((), ())), preferred_element_type=jnp.float32
        )
        return ((out_total, grad_buffer), contribution)

    carried = (
        jnp.zeros((row_count, model_width), jnp.float32),
        jnp.zeros(pre_gelu.shape, jnp.bfloat16),
    )

    def pass_weight(weight):
        return passed_along(weight, "blk", 1)

    def pass_grad(partial_value):
        return passed_along(partial_value, "blk", 1)

    carried, own_term = visit(down_weight, home_index * block_rows, carried)
    weight = pass_weight(down_weight)
    carried, contribution = visit(weight, jnp.mod(home_index - 1, cycle_size) * block_rows, carried)
    partial_value = contribution.astype(jnp.bfloat16)

    def one_stop(stop_number, loop_state):
        weight, partial_value, carried = loop_state
        weight = pass_weight(weight)
        carried, contribution = visit(
            weight, jnp.mod(home_index - stop_number, cycle_size) * block_rows, carried
        )
        partial_value = (pass_grad(partial_value).astype(jnp.float32) + contribution).astype(
            jnp.bfloat16
        )
        return (weight, partial_value, carried)

    weight, partial_value, carried = lax.fori_loop(
        2, cycle_size, one_stop, (weight, partial_value, carried)
    )
    finished = finish_partial(pass_grad(partial_value), own_term)
    out_total, grad_buffer = carried
    summed = lax.psum(finished.astype(jnp.bfloat16), "dp").astype(jnp.float32)
    token_count = row_count * cycle_size * lax.axis_size("dp")
    return (out_total.astype(jnp.bfloat16), grad_buffer, summed / math.sqrt(token_count))


def solution(mesh):
    in_specs = (P(("dp", "blk"), None), P(("dp", "blk"), None), P("blk", None))
    out_specs = (P(("dp", "blk"), None), P(("dp", "blk"), None), P("blk", None))
    return jax.shard_map(body, mesh=mesh, in_specs=in_specs, out_specs=out_specs, check_vma=False)
```

profile of v0, /device:TPU:1, one launch (start us, length us, event | category | flops | bytes accessed | tf_op | source)
XLA Modules:
  0.0 725.1 jit_solution(6232754334397640442)
XLA Ops:
  7.2 4.4 collective-permute-start.2
  11.6 4.5 fusion.14
  20.4 5.9 collective-permute-done.2
  28.4 498.7 %while.21 = (s32[]{:T(128)}, bf16[128,1024]{1,0:T(8,128)(2,1)S(1)}, bf16[128,1024]{1,0:T(8,128)(2,1)}, f32[192,1024]{1,0:T(8,128)S(1)}, bf16[192,4096]{1,0:T(8,1...) while((s32[]{:T(128)}, bf16[128,1024]{1,0:T(8,128)(2,1)S(1)}, ...), condition=%wide.region_1.2_spmd, body=%wide.region_0.1_spmd.sunk | while | flops 151633936 | bytes 6275492 | solution.py:84
  32.3 6.7 collective-permute-done
  39.3 5.3 collective-permute-done.1
  51.2 5.8 collective-permute-done
  57.3 5.3 collective-permute-done.1
  69.2 5.3 collective-permute-done
  74.9 4.8 collective-permute-done.1
  86.3 5.3 collective-permute-done
  91.9 3.9 collective-permute-done.1
  102.4 5.3 collective-permute-done
  108.1 3.0 collective-permute-done.1
  117.7 5.3 collective-permute-done
  123.3 2.5 collective-permute-done.1
  132.5 5.3 collective-permute-done
  138.1 2.5 collective-permute-done.1
  145.3 3.0 collective-permute-start.1
  148.3 4.2 collective-permute-done
  158.1 2.7 collective-permute-start
  160.9 4.0 collective-permute-start.1
  167.6 2.7 collective-permute-done.1
  173.1 3.9 collective-permute-start
  177.0 4.4 collective-permute-start.1
  183.0 3.4 collective-permute-done.1
  189.1 5.1 collective-permute-start
  194.2 4.0 collective-permute-start.1
  199.3 4.4 collective-permute-done.1
  206.4 4.5 collective-permute-start
  211.0 4.0 collective-permute-start.1
  215.9 4.5 collective-permute-done.1
  223.2 2.9 collective-permute-start
  226.1 4.0 collective-permute-start.1
  232.7 2.8 collective-permute-done.1
  240.2 4.0 collective-permute-start.1
  244.2 4.8 collective-permute-done
  258.5 8.2 %collective-permute-done = bf16[128,1024]{1,0:T(8,128)(2,1)S(1)} collective-permute-done((bf16[128,1024]{1,0:T(8,128)(2,1)S(1)}, bf16[128,1024]{1,0:T(8,128)(2,1)S(1)}, u32[]{:S(2)}, u32[]{:S(2)}) %collective-permute-start) | collective-permute-done | bytes 262176 | tf_op jit(solution)/shard_map/while/body/eval_jaxpr/ppermute | solution.py:13
  267.0 5.3 collective-permute-done.1
  278.9 7.3 %collective-permute-done = bf16[128,1024]{1,0:T(8,128)(2,1)S(1)} collective-permute-done((bf16[128,1024]{1,0:T(8,128)(2,1)S(1)}, bf16[128,1024]{1,0:T(8,128)(2,1)S(1)}, u32[]{:S(2)}, u32[]{:S(2)}) %collective-permute-start) | collective-permute-done | bytes 262176 | tf_op jit(solution)/shard_map/while/body/eval_jaxpr/ppermute | solution.py:13
  286.5 5.3 collective-permute-done.1
  298.5 6.4 collective-permute-done
  305.2 5.3 collective-permute-done.1
  317.1 5.3 collective-permute-done
  322.7 5.5 collective-permute-done.1
  334.8 5.3 collective-permute-done
  340.5 4.5 collective-permute-done.1
  351.6 5.3 collective-permute-done
  357.3 3.6 collective-permute-done.1
  367.5 5.3 collective-permute-done
  373.1 2.5 collective-permute-done.1
  382.3 5.5 collective-permute-done
  397.2 5.3 collective-permute-done
  412.0 5.3 collective-permute-done
  426.7 5.3 collective-permute-done
  441.5 6.3 collective-permute-done
  457.5 7.1 collective-permute-done
  474.0 8.5 %collective-permute-done = bf16[128,1024]{1,0:T(8,128)(2,1)S(1)} collective-permute-done((bf16[128,1024]{1,0:T(8,128)(2,1)S(1)}, bf16[128,1024]{1,0:T(8,128)(2,1)S(1)}, u32[]{:S(2)}, u32[]{:S(2)}) %collective-permute-start) | collective-permute-done | bytes 262176 | tf_op jit(solution)/shard_map/while/body/eval_jaxpr/ppermute | solution.py:13
  491.9 8.5 %collective-permute-done = bf16[128,1024]{1,0:T(8,128)(2,1)S(1)} collective-permute-done((bf16[128,1024]{1,0:T(8,128)(2,1)S(1)}, bf16[128,1024]{1,0:T(8,128)(2,1)S(1)}, u32[]{:S(2)}, u32[]{:S(2)}) %collective-permute-start) | collective-permute-done | bytes 262176 | tf_op jit(solution)/shard_map/while/body/eval_jaxpr/ppermute | solution.py:13
  500.7 3.5 collective-permute-done.1
  510.9 8.3 %collective-permute-done = bf16[128,1024]{1,0:T(8,128)(2,1)S(1)} collective-permute-done((bf16[128,1024]{1,0:T(8,128)(2,1)S(1)}, bf16[128,1024]{1,0:T(8,128)(2,1)S(1)}, u32[]{:S(2)}, u32[]{:S(2)}) %collective-permute-start) | collective-permute-done | bytes 262176 | tf_op jit(solution)/shard_map/while/body/eval_jaxpr/ppermute | solution.py:13
  519.5 4.8 collective-permute-done.1
  529.2 9.8 %collective-permute-done.3 = bf16[128,1024]{1,0:T(8,128)(2,1)S(1)} collective-permute-done((bf16[128,1024]{1,0:T(8,128)(2,1)}, bf16[128,1024]{1,0:T(8,128)(2,1)S(1)}, u32[]{:S(2)}, u32[]{:S(2)}) %collective-permute-start.3) | collective-permute-done | bytes 262176 | tf_op jit(solution)/shard_map/ppermute | solution.py:13
  540.6 175.8 %all-reduce.2.cloned.1.call-done = bf16[128,1024]{1,0:T(8,128)(2,1)} async-done(((bf16[128,1024]{1,0:T(8,128)(2,1)}), bf16[128,1024]{1,0:T(8,128)(2,1)}) %all-reduce.2.cloned.1.call-update) | async-done | bytes 262160 | tf_op jit(solution)/shard_map/psum | solution.py:89
  (199 shorter events, 225.2 us)
Async XLA Ops:
  7.2 709.2 %all-reduce.2.cloned.1.call-start = ((), (), s32[]{:S(2)}) async-start(), calls=%async_computation | async-start | bytes 524288 | tf_op jit(solution)/shard_map/psum | solution.py:89
  7.2 19.1 %collective-permute-start.2 = (bf16[128,1024]{1,0:T(8,128)(2,1)}, bf16[128,1024]{1,0:T(8,128)(2,1)S(1)}, u32[]{:S(2)}, u32[]{:S(2)}) collective-permute-start(bf16[128,1024]{1,0:T(8,128)(2,1)} %param.7), channel_id=1, source_target_pairs={{0,1},{1,2},{2,3},{3,4},{4,5},{5,6},{6,7},{7,8},{8,9},{9,10},{10,1... | collective-permute-start | bytes 786440 | tf_op jit(solution)/shard_map/ppermute | solution.py:13
  11.6 5.8 copy-start
  28.4 10.6 %collective-permute-start = (bf16[128,1024]{1,0:T(8,128)(2,1)S(1)}, bf16[128,1024]{1,0:T(8,128)(2,1)S(1)}, u32[]{:S(2)}, u32[]{:S(2)}) collective-permute-start(bf16[128,1024]{1,0:T(8,128)(2,1)S(1)} %get-tuple-element.321), channel_id=1, source_target_pairs={{0,1},{1,2},{2,3},{3,4},{4,5},{5,6},{6,7},{7,8},{8,9},{9,10},{10,1... | collective-permute-start | bytes 786440 | tf_op jit(solution)/shard_map/while/body/eval_jaxpr/ppermute | solution.py:13
  30.3 14.3 %collective-permute-start.1 = (bf16[128,1024]{1,0:T(8,128)(2,1)}, bf16[128,1024]{1,0:T(8,128)(2,1)S(1)}, u32[]{:S(2)}, u32[]{:S(2)}) collective-permute-start(bf16[128,1024]{1,0:T(8,128)(2,1)} %get-tuple-element.322), channel_id=1, source_target_pairs={{0,1},{1,2},{2,3},{3,4},{4,5},{5,6},{6,7},{7,8},{8,9},{9,10},{10,1... | collective-permute-start | bytes 786440 | tf_op jit(solution)/shard_map/while/body/eval_jaxpr/ppermute | solution.py:13
  47.3 9.6 %collective-permute-start = (bf16[128,1024]{1,0:T(8,128)(2,1)S(1)}, bf16[128,1024]{1,0:T(8,128)(2,1)S(1)}, u32[]{:S(2)}, u32[]{:S(2)}) collective-permute-start(bf16[128,1024]{1,0:T(8,128)(2,1)S(1)} %get-tuple-element.321), channel_id=1, source_target_pairs={{0,1},{1,2},{2,3},{3,4},{4,5},{5,6},{6,7},{7,8},{8,9},{9,10},{10,1... | collective-permute-start | bytes 786440 | tf_op jit(solution)/shard_map/while/body/eval_jaxpr/ppermute | solution.py:13
  49.3 13.3 %collective-permute-start.1 = (bf16[128,1024]{1,0:T(8,128)(2,1)}, bf16[128,1024]{1,0:T(8,128)(2,1)S(1)}, u32[]{:S(2)}, u32[]{:S(2)}) collective-permute-start(bf16[128,1024]{1,0:T(8,128)(2,1)} %get-tuple-element.322), channel_id=1, source_target_pairs={{0,1},{1,2},{2,3},{3,4},{4,5},{5,6},{6,7},{7,8},{8,9},{9,10},{10,1... | collective-permute-start | bytes 786440 | tf_op jit(solution)/shard_map/while/body/eval_jaxpr/ppermute | solution.py:13
  65.3 9.2 %collective-permute-start = (bf16[128,1024]{1,0:T(8,128)(2,1)S(1)}, bf16[128,1024]{1,0:T(8,128)(2,1)S(1)}, u32[]{:S(2)}, u32[]{:S(2)}) collective-permute-start(bf16[128,1024]{1,0:T(8,128)(2,1)S(1)} %get-tuple-element.321), channel_id=1, source_target_pairs={{0,1},{1,2},{2,3},{3,4},{4,5},{5,6},{6,7},{7,8},{8,9},{9,10},{10,1... | collective-permute-start | bytes 786440 | tf_op jit(solution)/shard_map/while/body/eval_jaxpr/ppermute | solution.py:13
  67.3 12.4 %collective-permute-start.1 = (bf16[128,1024]{1,0:T(8,128)(2,1)}, bf16[128,1024]{1,0:T(8,128)(2,1)S(1)}, u32[]{:S(2)}, u32[]{:S(2)}) collective-permute-start(bf16[128,1024]{1,0:T(8,128)(2,1)} %get-tuple-element.322), channel_id=1, source_target_pairs={{0,1},{1,2},{2,3},{3,4},{4,5},{5,6},{6,7},{7,8},{8,9},{9,10},{10,1... | collective-permute-start | bytes 786440 | tf_op jit(solution)/shard_map/while/body/eval_jaxpr/ppermute | solution.py:13
  82.4 9.2 %collective-permute-start = (bf16[128,1024]{1,0:T(8,128)(2,1)S(1)}, bf16[128,1024]{1,0:T(8,128)(2,1)S(1)}, u32[]{:S(2)}, u32[]{:S(2)}) collective-permute-start(bf16[128,1024]{1,0:T(8,128)(2,1)S(1)} %get-tuple-element.321), channel_id=1, source_target_pairs={{0,1},{1,2},{2,3},{3,4},{4,5},{5,6},{6,7},{7,8},{8,9},{9,10},{10,1... | collective-permute-start | bytes 786440 | tf_op jit(solution)/shard_map/while/body/eval_jaxpr/ppermute | solution.py:13
  84.3 11.5 %collective-permute-start.1 = (bf16[128,1024]{1,0:T(8,128)(2,1)}, bf16[128,1024]{1,0:T(8,128)(2,1)S(1)}, u32[]{:S(2)}, u32[]{:S(2)}) collective-permute-start(bf16[128,1024]{1,0:T(8,128)(2,1)} %get-tuple-element.322), channel_id=1, source_target_pairs={{0,1},{1,2},{2,3},{3,4},{4,5},{5,6},{6,7},{7,8},{8,9},{9,10},{10,1... | collective-permute-start | bytes 786440 | tf_op jit(solution)/shard_map/while/body/eval_jaxpr/ppermute | solution.py:13
  98.6 9.2 %collective-permute-start = (bf16[128,1024]{1,0:T(8,128)(2,1)S(1)}, bf16[128,1024]{1,0:T(8,128)(2,1)S(1)}, u32[]{:S(2)}, u32[]{:S(2)}) collective-permute-start(bf16[128,1024]{1,0:T(8,128)(2,1)S(1)} %get-tuple-element.321), channel_id=1, source_target_pairs={{0,1},{1,2},{2,3},{3,4},{4,5},{5,6},{6,7},{7,8},{8,9},{9,10},{10,1... | collective-permute-start | bytes 786440 | tf_op jit(solution)/shard_map/while/body/eval_jaxpr/ppermute | solution.py:13
  100.5 10.6 %collective-permute-start.1 = (bf16[128,1024]{1,0:T(8,128)(2,1)}, bf16[128,1024]{1,0:T(8,128)(2,1)S(1)}, u32[]{:S(2)}, u32[]{:S(2)}) collective-permute-start(bf16[128,1024]{1,0:T(8,128)(2,1)} %get-tuple-element.322), channel_id=1, source_target_pairs={{0,1},{1,2},{2,3},{3,4},{4,5},{5,6},{6,7},{7,8},{8,9},{9,10},{10,1... | collective-permute-start | bytes 786440 | tf_op jit(solution)/shard_map/while/body/eval_jaxpr/ppermute | solution.py:13
  113.8 9.2 %collective-permute-start = (bf16[128,1024]{1,0:T(8,128)(2,1)S(1)}, bf16[128,1024]{1,0:T(8,128)(2,1)S(1)}, u32[]{:S(2)}, u32[]{:S(2)}) collective-permute-start(bf16[128,1024]{1,0:T(8,128)(2,1)S(1)} %get-tuple-element.321), channel_id=1, source_target_pairs={{0,1},{1,2},{2,3},{3,4},{4,5},{5,6},{6,7},{7,8},{8,9},{9,10},{10,1... | collective-permute-start | bytes 786440 | tf_op jit(solution)/shard_map/while/body/eval_jaxpr/ppermute | solution.py:13
  115.7 10.1 %collective-permute-start.1 = (bf16[128,1024]{1,0:T(8,128)(2,1)}, bf16[128,1024]{1,0:T(8,128)(2,1)S(1)}, u32[]{:S(2)}, u32[]{:S(2)}) collective-permute-start(bf16[128,1024]{1,0:T(8,128)(2,1)} %get-tuple-element.322), channel_id=1, source_target_pairs={{0,1},{1,2},{2,3},{3,4},{4,5},{5,6},{6,7},{7,8},{8,9},{9,10},{10,1... | collective-permute-start | bytes 786440 | tf_op jit(solution)/shard_map/while/body/eval_jaxpr/ppermute | solution.py:13
  128.6 9.2 %collective-permute-start = (bf16[128,1024]{1,0:T(8,128)(2,1)S(1)}, bf16[128,1024]{1,0:T(8,128)(2,1)S(1)}, u32[]{:S(2)}, u32[]{:S(2)}) collective-permute-start(bf16[128,1024]{1,0:T(8,128)(2,1)S(1)} %get-tuple-element.321), channel_id=1, source_target_pairs={{0,1},{1,2},{2,3},{3,4},{4,5},{5,6},{6,7},{7,8},{8,9},{9,10},{10,1... | collective-permute-start | bytes 786440 | tf_op jit(solution)/shard_map/while/body/eval_jaxpr/ppermute | solution.py:13
  130.5 10.1 %collective-permute-start.1 = (bf16[128,1024]{1,0:T(8,128)(2,1)}, bf16[128,1024]{1,0:T(8,128)(2,1)S(1)}, u32[]{:S(2)}, u32[]{:S(2)}) collective-permute-start(bf16[128,1024]{1,0:T(8,128)(2,1)} %get-tuple-element.322), channel_id=1, source_target_pairs={{0,1},{1,2},{2,3},{3,4},{4,5},{5,6},{6,7},{7,8},{8,9},{9,10},{10,1... | collective-permute-start | bytes 786440 | tf_op jit(solution)/shard_map/while/body/eval_jaxpr/ppermute | solution.py:13
  143.4 9.2 %collective-permute-start = (bf16[128,1024]{1,0:T(8,128)(2,1)S(1)}, bf16[128,1024]{1,0:T(8,128)(2,1)S(1)}, u32[]{:S(2)}, u32[]{:S(2)}) collective-permute-start(bf16[128,1024]{1,0:T(8,128)(2,1)S(1)} %get-tuple-element.321), channel_id=1, source_target_pairs={{0,1},{1,2},{2,3},{3,4},{4,5},{5,6},{6,7},{7,8},{8,9},{9,10},{10,1... | collective-permute-start | bytes 786440 | tf_op jit(solution)/shard_map/while/body/eval_jaxpr/ppermute | solution.py:13
  145.3 10.1 %collective-permute-start.1 = (bf16[128,1024]{1,0:T(8,128)(2,1)}, bf16[128,1024]{1,0:T(8,128)(2,1)S(1)}, u32[]{:S(2)}, u32[]{:S(2)}) collective-permute-start(bf16[128,1024]{1,0:T(8,128)(2,1)} %get-tuple-element.322), channel_id=1, source_target_pairs={{0,1},{1,2},{2,3},{3,4},{4,5},{5,6},{6,7},{7,8},{8,9},{9,10},{10,1... | collective-permute-start | bytes 786440 | tf_op jit(solution)/shard_map/while/body/eval_jaxpr/ppermute | solution.py:13
  158.1 9.2 %collective-permute-start = (bf16[128,1024]{1,0:T(8,128)(2,1)S(1)}, bf16[128,1024]{1,0:T(8,128)(2,1)S(1)}, u32[]{:S(2)}, u32[]{:S(2)}) collective-permute-start(bf16[128,1024]{1,0:T(8,128)(2,1)S(1)} %get-tuple-element.321), channel_id=1, source_target_pairs={{0,1},{1,2},{2,3},{3,4},{4,5},{5,6},{6,7},{7,8},{8,9},{9,10},{10,1... | collective-permute-start | bytes 786440 | tf_op jit(solution)/shard_map/while/body/eval_jaxpr/ppermute | solution.py:13
  160.9 9.4 %collective-permute-start.1 = (bf16[128,1024]{1,0:T(8,128)(2,1)}, bf16[128,1024]{1,0:T(8,128)(2,1)S(1)}, u32[]{:S(2)}, u32[]{:S(2)}) collective-permute-start(bf16[128,1024]{1,0:T(8,128)(2,1)} %get-tuple-element.322), channel_id=1, source_target_pairs={{0,1},{1,2},{2,3},{3,4},{4,5},{5,6},{6,7},{7,8},{8,9},{9,10},{10,1... | collective-permute-start | bytes 786440 | tf_op jit(solution)/shard_map/while/body/eval_jaxpr/ppermute | solution.py:13
  173.1 9.6 %collective-permute-start = (bf16[128,1024]{1,0:T(8,128)(2,1)S(1)}, bf16[128,1024]{1,0:T(8,128)(2,1)S(1)}, u32[]{:S(2)}, u32[]{:S(2)}) collective-permute-start(bf16[128,1024]{1,0:T(8,128)(2,1)S(1)} %get-tuple-element.321), channel_id=1, source_target_pairs={{0,1},{1,2},{2,3},{3,4},{4,5},{5,6},{6,7},{7,8},{8,9},{9,10},{10,1... | collective-permute-start | bytes 786440 | tf_op jit(solution)/shard_map/while/body/eval_jaxpr/ppermute | solution.py:13
  177.0 9.4 %collective-permute-start.1 = (bf16[128,1024]{1,0:T(8,128)(2,1)}, bf16[128,1024]{1,0:T(8,128)(2,1)S(1)}, u32[]{:S(2)}, u32[]{:S(2)}) collective-permute-start(bf16[128,1024]{1,0:T(8,128)(2,1)} %get-tuple-element.322), channel_id=1, source_target_pairs={{0,1},{1,2},{2,3},{3,4},{4,5},{5,6},{6,7},{7,8},{8,9},{9,10},{10,1... | collective-permute-start | bytes 786440 | tf_op jit(solution)/shard_map/while/body/eval_jaxpr/ppermute | solution.py:13
  189.1 9.9 %collective-permute-start = (bf16[128,1024]{1,0:T(8,128)(2,1)S(1)}, bf16[128,1024]{1,0:T(8,128)(2,1)S(1)}, u32[]{:S(2)}, u32[]{:S(2)}) collective-permute-start(bf16[128,1024]{1,0:T(8,128)(2,1)S(1)} %get-tuple-element.321), channel_id=1, source_target_pairs={{0,1},{1,2},{2,3},{3,4},{4,5},{5,6},{6,7},{7,8},{8,9},{9,10},{10,1... | collective-permute-start | bytes 786440 | tf_op jit(solution)/shard_map/while/body/eval_jaxpr/ppermute | solution.py:13
  194.2 9.4 %collective-permute-start.1 = (bf16[128,1024]{1,0:T(8,128)(2,1)}, bf16[128,1024]{1,0:T(8,128)(2,1)S(1)}, u32[]{:S(2)}, u32[]{:S(2)}) collective-permute-start(bf16[128,1024]{1,0:T(8,128)(2,1)} %get-tuple-element.322), channel_id=1, source_target_pairs={{0,1},{1,2},{2,3},{3,4},{4,5},{5,6},{6,7},{7,8},{8,9},{9,10},{10,1... | collective-permute-start | bytes 786440 | tf_op jit(solution)/shard_map/while/body/eval_jaxpr/ppermute | solution.py:13
  206.4 9.2 %collective-permute-start = (bf16[128,1024]{1,0:T(8,128)(2,1)S(1)}, bf16[128,1024]{1,0:T(8,128)(2,1)S(1)}, u32[]{:S(2)}, u32[]{:S(2)}) collective-permute-start(bf16[128,1024]{1,0:T(8,128)(2,1)S(1)} %get-tuple-element.321), channel_id=1, source_target_pairs={{0,1},{1,2},{2,3},{3,4},{4,5},{5,6},{6,7},{7,8},{8,9},{9,10},{10,1... | collective-permute-start | bytes 786440 | tf_op jit(solution)/shard_map/while/body/eval_jaxpr/ppermute | solution.py:13
  211.0 9.4 %collective-permute-start.1 = (bf16[128,1024]{1,0:T(8,128)(2,1)}, bf16[128,1024]{1,0:T(8,128)(2,1)S(1)}, u32[]{:S(2)}, u32[]{:S(2)}) collective-permute-start(bf16[128,1024]{1,0:T(8,128)(2,1)} %get-tuple-element.322), channel_id=1, source_target_pairs={{0,1},{1,2},{2,3},{3,4},{4,5},{5,6},{6,7},{7,8},{8,9},{9,10},{10,1... | collective-permute-start | bytes 786440 | tf_op jit(solution)/shard_map/while/body/eval_jaxpr/ppermute | solution.py:13
  223.2 9.2 %collective-permute-start = (bf16[128,1024]{1,0:T(8,128)(2,1)S(1)}, bf16[128,1024]{1,0:T(8,128)(2,1)S(1)}, u32[]{:S(2)}, u32[]{:S(2)}) collective-permute-start(bf16[128,1024]{1,0:T(8,128)(2,1)S(1)} %get-tuple-element.321), channel_id=1, source_target_pairs={{0,1},{1,2},{2,3},{3,4},{4,5},{5,6},{6,7},{7,8},{8,9},{9,10},{10,1... | collective-permute-start | bytes 786440 | tf_op jit(solution)/shard_map/while/body/eval_jaxpr/ppermute | solution.py:13
  226.1 9.4 %collective-permute-start.1 = (bf16[128,1024]{1,0:T(8,128)(2,1)}, bf16[128,1024]{1,0:T(8,128)(2,1)S(1)}, u32[]{:S(2)}, u32[]{:S(2)}) collective-permute-start(bf16[128,1024]{1,0:T(8,128)(2,1)} %get-tuple-element.322), channel_id=1, source_target_pairs={{0,1},{1,2},{2,3},{3,4},{4,5},{5,6},{6,7},{7,8},{8,9},{9,10},{10,1... | collective-permute-start | bytes 786440 | tf_op jit(solution)/shard_map/while/body/eval_jaxpr/ppermute | solution.py:13
  238.2 10.8 %collective-permute-start = (bf16[128,1024]{1,0:T(8,128)(2,1)S(1)}, bf16[128,1024]{1,0:T(8,128)(2,1)S(1)}, u32[]{:S(2)}, u32[]{:S(2)}) collective-permute-start(bf16[128,1024]{1,0:T(8,128)(2,1)S(1)} %get-tuple-element.321), channel_id=1, source_target_pairs={{0,1},{1,2},{2,3},{3,4},{4,5},{5,6},{6,7},{7,8},{8,9},{9,10},{10,1... | collective-permute-start | bytes 786440 | tf_op jit(solution)/shard_map/while/body/eval_jaxpr/ppermute | solution.py:13
  240.2 11.6 %collective-permute-start.1 = (bf16[128,1024]{1,0:T(8,128)(2,1)}, bf16[128,1024]{1,0:T(8,128)(2,1)S(1)}, u32[]{:S(2)}, u32[]{:S(2)}) collective-permute-start(bf16[128,1024]{1,0:T(8,128)(2,1)} %get-tuple-element.322), channel_id=1, source_target_pairs={{0,1},{1,2},{2,3},{3,4},{4,5},{5,6},{6,7},{7,8},{8,9},{9,10},{10,1... | collective-permute-start | bytes 786440 | tf_op jit(solution)/shard_map/while/body/eval_jaxpr/ppermute | solution.py:13
  254.6 12.1 %collective-permute-start = (bf16[128,1024]{1,0:T(8,128)(2,1)S(1)}, bf16[128,1024]{1,0:T(8,128)(2,1)S(1)}, u32[]{:S(2)}, u32[]{:S(2)}) collective-permute-start(bf16[128,1024]{1,0:T(8,128)(2,1)S(1)} %get-tuple-element.321), channel_id=1, source_target_pairs={{0,1},{1,2},{2,3},{3,4},{4,5},{5,6},{6,7},{7,8},{8,9},{9,10},{10,1... | collective-permute-start | bytes 786440 | tf_op jit(solution)/shard_map/while/body/eval_jaxpr/ppermute | solution.py:13
  256.5 15.8 %collective-permute-start.1 = (bf16[128,1024]{1,0:T(8,128)(2,1)}, bf16[128,1024]{1,0:T(8,128)(2,1)S(1)}, u32[]{:S(2)}, u32[]{:S(2)}) collective-permute-start(bf16[128,1024]{1,0:T(8,128)(2,1)} %get-tuple-element.322), channel_id=1, source_target_pairs={{0,1},{1,2},{2,3},{3,4},{4,5},{5,6},{6,7},{7,8},{8,9},{9,10},{10,1... | collective-permute-start | bytes 786440 | tf_op jit(solution)/shard_map/while/body/eval_jaxpr/ppermute | solution.py:13
  275.0 11.2 %collective-permute-start = (bf16[128,1024]{1,0:T(8,128)(2,1)S(1)}, bf16[128,1024]{1,0:T(8,128)(2,1)S(1)}, u32[]{:S(2)}, u32[]{:S(2)}) collective-permute-start(bf16[128,1024]{1,0:T(8,128)(2,1)S(1)} %get-tuple-element.321), channel_id=1, source_target_pairs={{0,1},{1,2},{2,3},{3,4},{4,5},{5,6},{6,7},{7,8},{8,9},{9,10},{10,1... | collective-permute-start | bytes 786440 | tf_op jit(solution)/shard_map/while/body/eval_jaxpr/ppermute | solution.py:13
  276.9 14.9 %collective-permute-start.1 = (bf16[128,1024]{1,0:T(8,128)(2,1)}, bf16[128,1024]{1,0:T(8,128)(2,1)S(1)}, u32[]{:S(2)}, u32[]{:S(2)}) collective-permute-start(bf16[128,1024]{1,0:T(8,128)(2,1)} %get-tuple-element.322), channel_id=1, source_target_pairs={{0,1},{1,2},{2,3},{3,4},{4,5},{5,6},{6,7},{7,8},{8,9},{9,10},{10,1... | collective-permute-start | bytes 786440 | tf_op jit(solution)/shard_map/while/body/eval_jaxpr/ppermute | solution.py:13
  294.6 10.3 %collective-permute-start = (bf16[128,1024]{1,0:T(8,128)(2,1)S(1)}, bf16[128,1024]{1,0:T(8,128)(2,1)S(1)}, u32[]{:S(2)}, u32[]{:S(2)}) collective-permute-start(bf16[128,1024]{1,0:T(8,128)(2,1)S(1)} %get-tuple-element.321), channel_id=1, source_target_pairs={{0,1},{1,2},{2,3},{3,4},{4,5},{5,6},{6,7},{7,8},{8,9},{9,10},{10,1... | collective-permute-start | bytes 786440 | tf_op jit(solution)/shard_map/while/body/eval_jaxpr/ppermute | solution.py:13
  296.5 14.0 %collective-permute-start.1 = (bf16[128,1024]{1,0:T(8,128)(2,1)}, bf16[128,1024]{1,0:T(8,128)(2,1)S(1)}, u32[]{:S(2)}, u32[]{:S(2)}) collective-permute-start(bf16[128,1024]{1,0:T(8,128)(2,1)} %get-tuple-element.322), channel_id=1, source_target_pairs={{0,1},{1,2},{2,3},{3,4},{4,5},{5,6},{6,7},{7,8},{8,9},{9,10},{10,1... | collective-permute-start | bytes 786440 | tf_op jit(solution)/shard_map/while/body/eval_jaxpr/ppermute | solution.py:13
  313.2 9.2 %collective-permute-start = (bf16[128,1024]{1,0:T(8,128)(2,1)S(1)}, bf16[128,1024]{1,0:T(8,128)(2,1)S(1)}, u32[]{:S(2)}, u32[]{:S(2)}) collective-permute-start(bf16[128,1024]{1,0:T(8,128)(2,1)S(1)} %get-tuple-element.321), channel_id=1, source_target_pairs={{0,1},{1,2},{2,3},{3,4},{4,5},{5,6},{6,7},{7,8},{8,9},{9,10},{10,1... | collective-permute-start | bytes 786440 | tf_op jit(solution)/shard_map/while/body/eval_jaxpr/ppermute | solution.py:13
  315.1 13.1 %collective-permute-start.1 = (bf16[128,1024]{1,0:T(8,128)(2,1)}, bf16[128,1024]{1,0:T(8,128)(2,1)S(1)}, u32[]{:S(2)}, u32[]{:S(2)}) collective-permute-start(bf16[128,1024]{1,0:T(8,128)(2,1)} %get-tuple-element.322), channel_id=1, source_target_pairs={{0,1},{1,2},{2,3},{3,4},{4,5},{5,6},{6,7},{7,8},{8,9},{9,10},{10,1... | collective-permute-start | bytes 786440 | tf_op jit(solution)/shard_map/while/body/eval_jaxpr/ppermute | solution.py:13
  330.9 9.2 %collective-permute-start = (bf16[128,1024]{1,0:T(8,128)(2,1)S(1)}, bf16[128,1024]{1,0:T(8,128)(2,1)S(1)}, u32[]{:S(2)}, u32[]{:S(2)}) collective-permute-start(bf16[128,1024]{1,0:T(8,128)(2,1)S(1)} %get-tuple-element.321), channel_id=1, source_target_pairs={{0,1},{1,2},{2,3},{3,4},{4,5},{5,6},{6,7},{7,8},{8,9},{9,10},{10,1... | collective-permute-start | bytes 786440 | tf_op jit(solution)/shard_map/while/body/eval_jaxpr/ppermute | solution.py:13
  332.9 12.1 %collective-permute-start.1 = (bf16[128,1024]{1,0:T(8,128)(2,1)}, bf16[128,1024]{1,0:T(8,128)(2,1)S(1)}, u32[]{:S(2)}, u32[]{:S(2)}) collective-permute-start(bf16[128,1024]{1,0:T(8,128)(2,1)} %get-tuple-element.322), channel_id=1, source_target_pairs={{0,1},{1,2},{2,3},{3,4},{4,5},{5,6},{6,7},{7,8},{8,9},{9,10},{10,1... | collective-permute-start | bytes 786440 | tf_op jit(solution)/shard_map/while/body/eval_jaxpr/ppermute | solution.py:13
  347.7 9.2 %collective-permute-start = (bf16[128,1024]{1,0:T(8,128)(2,1)S(1)}, bf16[128,1024]{1,0:T(8,128)(2,1)S(1)}, u32[]{:S(2)}, u32[]{:S(2)}) collective-permute-start(bf16[128,1024]{1,0:T(8,128)(2,1)S(1)} %get-tuple-element.321), channel_id=1, source_target_pairs={{0,1},{1,2},{2,3},{3,4},{4,5},{5,6},{6,7},{7,8},{8,9},{9,10},{10,1... | collective-permute-start | bytes 786440 | tf_op jit(solution)/shard_map/while/body/eval_jaxpr/ppermute | solution.py:13
  349.7 11.2 %collective-permute-start.1 = (bf16[128,1024]{1,0:T(8,128)(2,1)}, bf16[128,1024]{1,0:T(8,128)(2,1)S(1)}, u32[]{:S(2)}, u32[]{:S(2)}) collective-permute-start(bf16[128,1024]{1,0:T(8,128)(2,1)} %get-tuple-element.322), channel_id=1, source_target_pairs={{0,1},{1,2},{2,3},{3,4},{4,5},{5,6},{6,7},{7,8},{8,9},{9,10},{10,1... | collective-permute-start | bytes 786440 | tf_op jit(solution)/shard_map/while/body/eval_jaxpr/ppermute | solution.py:13
  363.6 9.2 %collective-permute-start = (bf16[128,1024]{1,0:T(8,128)(2,1)S(1)}, bf16[128,1024]{1,0:T(8,128)(2,1)S(1)}, u32[]{:S(2)}, u32[]{:S(2)}) collective-permute-start(bf16[128,1024]{1,0:T(8,128)(2,1)S(1)} %get-tuple-element.321), channel_id=1, source_target_pairs={{0,1},{1,2},{2,3},{3,4},{4,5},{5,6},{6,7},{7,8},{8,9},{9,10},{10,1... | collective-permute-start | bytes 786440 | tf_op jit(solution)/shard_map/while/body/eval_jaxpr/ppermute | solution.py:13
  365.5 10.1 %collective-permute-start.1 = (bf16[128,1024]{1,0:T(8,128)(2,1)}, bf16[128,1024]{1,0:T(8,128)(2,1)S(1)}, u32[]{:S(2)}, u32[]{:S(2)}) collective-permute-start(bf16[128,1024]{1,0:T(8,128)(2,1)} %get-tuple-element.322), channel_id=1, source_target_pairs={{0,1},{1,2},{2,3},{3,4},{4,5},{5,6},{6,7},{7,8},{8,9},{9,10},{10,1... | collective-permute-start | bytes 786440 | tf_op jit(solution)/shard_map/while/body/eval_jaxpr/ppermute | solution.py:13
  378.4 9.4 %collective-permute-start = (bf16[128,1024]{1,0:T(8,128)(2,1)S(1)}, bf16[128,1024]{1,0:T(8,128)(2,1)S(1)}, u32[]{:S(2)}, u32[]{:S(2)}) collective-permute-start(bf16[128,1024]{1,0:T(8,128)(2,1)S(1)} %get-tuple-element.321), channel_id=1, source_target_pairs={{0,1},{1,2},{2,3},{3,4},{4,5},{5,6},{6,7},{7,8},{8,9},{9,10},{10,1... | collective-permute-start | bytes 786440 | tf_op jit(solution)/shard_map/while/body/eval_jaxpr/ppermute | solution.py:13
  380.3 10.3 %collective-permute-start.1 = (bf16[128,1024]{1,0:T(8,128)(2,1)}, bf16[128,1024]{1,0:T(8,128)(2,1)S(1)}, u32[]{:S(2)}, u32[]{:S(2)}) collective-permute-start(bf16[128,1024]{1,0:T(8,128)(2,1)} %get-tuple-element.322), channel_id=1, source_target_pairs={{0,1},{1,2},{2,3},{3,4},{4,5},{5,6},{6,7},{7,8},{8,9},{9,10},{10,1... | collective-permute-start | bytes 786440 | tf_op jit(solution)/shard_map/while/body/eval_jaxpr/ppermute | solution.py:13
  393.3 9.2 %collective-permute-start = (bf16[128,1024]{1,0:T(8,128)(2,1)S(1)}, bf16[128,1024]{1,0:T(8,128)(2,1)S(1)}, u32[]{:S(2)}, u32[]{:S(2)}) collective-permute-start(bf16[128,1024]{1,0:T(8,128)(2,1)S(1)} %get-tuple-element.321), channel_id=1, source_target_pairs={{0,1},{1,2},{2,3},{3,4},{4,5},{5,6},{6,7},{7,8},{8,9},{9,10},{10,1... | collective-permute-start | bytes 786440 | tf_op jit(solution)/shard_map/while/body/eval_jaxpr/ppermute | solution.py:13
  395.2 10.1 %collective-permute-start.1 = (bf16[128,1024]{1,0:T(8,128)(2,1)}, bf16[128,1024]{1,0:T(8,128)(2,1)S(1)}, u32[]{:S(2)}, u32[]{:S(2)}) collective-permute-start(bf16[128,1024]{1,0:T(8,128)(2,1)} %get-tuple-element.322), channel_id=1, source_target_pairs={{0,1},{1,2},{2,3},{3,4},{4,5},{5,6},{6,7},{7,8},{8,9},{9,10},{10,1... | collective-permute-start | bytes 786440 | tf_op jit(solution)/shard_map/while/body/eval_jaxpr/ppermute | solution.py:13
  408.1 9.2 %collective-permute-start = (bf16[128,1024]{1,0:T(8,128)(2,1)S(1)}, bf16[128,1024]{1,0:T(8,128)(2,1)S(1)}, u32[]{:S(2)}, u32[]{:S(2)}) collective-permute-start(bf16[128,1024]{1,0:T(8,128)(2,1)S(1)} %get-tuple-element.321), channel_id=1, source_target_pairs={{0,1},{1,2},{2,3},{3,4},{4,5},{5,6},{6,7},{7,8},{8,9},{9,10},{10,1... | collective-permute-start | bytes 786440 | tf_op jit(solution)/shard_map/while/body/eval_jaxpr/ppermute | solution.py:13
  410.0 10.1 %collective-permute-start.1 = (bf16[128,1024]{1,0:T(8,128)(2,1)}, bf16[128,1024]{1,0:T(8,128)(2,1)S(1)}, u32[]{:S(2)}, u32[]{:S(2)}) collective-permute-start(bf16[128,1024]{1,0:T(8,128)(2,1)} %get-tuple-element.322), channel_id=1, source_target_pairs={{0,1},{1,2},{2,3},{3,4},{4,5},{5,6},{6,7},{7,8},{8,9},{9,10},{10,1... | collective-permute-start | bytes 786440 | tf_op jit(solution)/shard_map/while/body/eval_jaxpr/ppermute | solution.py:13
  422.9 9.2 %collective-permute-start = (bf16[128,1024]{1,0:T(8,128)(2,1)S(1)}, bf16[128,1024]{1,0:T(8,128)(2,1)S(1)}, u32[]{:S(2)}, u32[]{:S(2)}) collective-permute-start(bf16[128,1024]{1,0:T(8,128)(2,1)S(1)} %get-tuple-element.321), channel_id=1, source_target_pairs={{0,1},{1,2},{2,3},{3,4},{4,5},{5,6},{6,7},{7,8},{8,9},{9,10},{10,1... | collective-permute-start | bytes 786440 | tf_op jit(solution)/shard_map/while/body/eval_jaxpr/ppermute | solution.py:13
  424.8 10.1 %collective-permute-start.1 = (bf16[128,1024]{1,0:T(8,128)(2,1)}, bf16[128,1024]{1,0:T(8,128)(2,1)S(1)}, u32[]{:S(2)}, u32[]{:S(2)}) collective-permute-start(bf16[128,1024]{1,0:T(8,128)(2,1)} %get-tuple-element.322), channel_id=1, source_target_pairs={{0,1},{1,2},{2,3},{3,4},{4,5},{5,6},{6,7},{7,8},{8,9},{9,10},{10,1... | collective-permute-start | bytes 786440 | tf_op jit(solution)/shard_map/while/body/eval_jaxpr/ppermute | solution.py:13
  437.6 10.2 %collective-permute-start = (bf16[128,1024]{1,0:T(8,128)(2,1)S(1)}, bf16[128,1024]{1,0:T(8,128)(2,1)S(1)}, u32[]{:S(2)}, u32[]{:S(2)}) collective-permute-start(bf16[128,1024]{1,0:T(8,128)(2,1)S(1)} %get-tuple-element.321), channel_id=1, source_target_pairs={{0,1},{1,2},{2,3},{3,4},{4,5},{5,6},{6,7},{7,8},{8,9},{9,10},{10,1... | collective-permute-start | bytes 786440 | tf_op jit(solution)/shard_map/while/body/eval_jaxpr/ppermute | solution.py:13
  439.5 11.1 %collective-permute-start.1 = (bf16[128,1024]{1,0:T(8,128)(2,1)}, bf16[128,1024]{1,0:T(8,128)(2,1)S(1)}, u32[]{:S(2)}, u32[]{:S(2)}) collective-permute-start(bf16[128,1024]{1,0:T(8,128)(2,1)} %get-tuple-element.322), channel_id=1, source_target_pairs={{0,1},{1,2},{2,3},{3,4},{4,5},{5,6},{6,7},{7,8},{8,9},{9,10},{10,1... | collective-permute-start | bytes 786440 | tf_op jit(solution)/shard_map/while/body/eval_jaxpr/ppermute | solution.py:13
  453.4 11.2 %collective-permute-start = (bf16[128,1024]{1,0:T(8,128)(2,1)S(1)}, bf16[128,1024]{1,0:T(8,128)(2,1)S(1)}, u32[]{:S(2)}, u32[]{:S(2)}) collective-permute-start(bf16[128,1024]{1,0:T(8,128)(2,1)S(1)} %get-tuple-element.321), channel_id=1, source_target_pairs={{0,1},{1,2},{2,3},{3,4},{4,5},{5,6},{6,7},{7,8},{8,9},{9,10},{10,1... | collective-permute-start | bytes 786440 | tf_op jit(solution)/shard_map/while/body/eval_jaxpr/ppermute | solution.py:13
  455.3 12.1 %collective-permute-start.1 = (bf16[128,1024]{1,0:T(8,128)(2,1)}, bf16[128,1024]{1,0:T(8,128)(2,1)S(1)}, u32[]{:S(2)}, u32[]{:S(2)}) collective-permute-start(bf16[128,1024]{1,0:T(8,128)(2,1)} %get-tuple-element.322), channel_id=1, source_target_pairs={{0,1},{1,2},{2,3},{3,4},{4,5},{5,6},{6,7},{7,8},{8,9},{9,10},{10,1... | collective-permute-start | bytes 786440 | tf_op jit(solution)/shard_map/while/body/eval_jaxpr/ppermute | solution.py:13
  470.2 12.4 %collective-permute-start = (bf16[128,1024]{1,0:T(8,128)(2,1)S(1)}, bf16[128,1024]{1,0:T(8,128)(2,1)S(1)}, u32[]{:S(2)}, u32[]{:S(2)}) collective-permute-start(bf16[128,1024]{1,0:T(8,128)(2,1)S(1)} %get-tuple-element.321), channel_id=1, source_target_pairs={{0,1},{1,2},{2,3},{3,4},{4,5},{5,6},{6,7},{7,8},{8,9},{9,10},{10,1... | collective-permute-start | bytes 786440 | tf_op jit(solution)/shard_map/while/body/eval_jaxpr/ppermute | solution.py:13
  472.1 13.2 %collective-permute-start.1 = (bf16[128,1024]{1,0:T(8,128)(2,1)}, bf16[128,1024]{1,0:T(8,128)(2,1)S(1)}, u32[]{:S(2)}, u32[]{:S(2)}) collective-permute-start(bf16[128,1024]{1,0:T(8,128)(2,1)} %get-tuple-element.322), channel_id=1, source_target_pairs={{0,1},{1,2},{2,3},{3,4},{4,5},{5,6},{6,7},{7,8},{8,9},{9,10},{10,1... | collective-permute-start | bytes 786440 | tf_op jit(solution)/shard_map/while/body/eval_jaxpr/ppermute | solution.py:13
  488.0 12.4 %collective-permute-start = (bf16[128,1024]{1,0:T(8,128)(2,1)S(1)}, bf16[128,1024]{1,0:T(8,128)(2,1)S(1)}, u32[]{:S(2)}, u32[]{:S(2)}) collective-permute-start(bf16[128,1024]{1,0:T(8,128)(2,1)S(1)} %get-tuple-element.321), channel_id=1, source_target_pairs={{0,1},{1,2},{2,3},{3,4},{4,5},{5,6},{6,7},{7,8},{8,9},{9,10},{10,1... | collective-permute-start | bytes 786440 | tf_op jit(solution)/shard_map/while/body/eval_jaxpr/ppermute | solution.py:13
  489.9 14.3 %collective-permute-start.1 = (bf16[128,1024]{1,0:T(8,128)(2,1)}, bf16[128,1024]{1,0:T(8,128)(2,1)S(1)}, u32[]{:S(2)}, u32[]{:S(2)}) collective-permute-start(bf16[128,1024]{1,0:T(8,128)(2,1)} %get-tuple-element.322), channel_id=1, source_target_pairs={{0,1},{1,2},{2,3},{3,4},{4,5},{5,6},{6,7},{7,8},{8,9},{9,10},{10,1... | collective-permute-start | bytes 786440 | tf_op jit(solution)/shard_map/while/body/eval_jaxpr/ppermute | solution.py:13
  507.0 12.2 %collective-permute-start = (bf16[128,1024]{1,0:T(8,128)(2,1)S(1)}, bf16[128,1024]{1,0:T(8,128)(2,1)S(1)}, u32[]{:S(2)}, u32[]{:S(2)}) collective-permute-start(bf16[128,1024]{1,0:T(8,128)(2,1)S(1)} %get-tuple-element.321), channel_id=1, source_target_pairs={{0,1},{1,2},{2,3},{3,4},{4,5},{5,6},{6,7},{7,8},{8,9},{9,10},{10,1... | collective-permute-start | bytes 786440 | tf_op jit(solution)/shard_map/while/body/eval_jaxpr/ppermute | solution.py:13
  508.9 15.4 %collective-permute-start.1 = (bf16[128,1024]{1,0:T(8,128)(2,1)}, bf16[128,1024]{1,0:T(8,128)(2,1)S(1)}, u32[]{:S(2)}, u32[]{:S(2)}) collective-permute-start(bf16[128,1024]{1,0:T(8,128)(2,1)} %get-tuple-element.322), channel_id=1, source_target_pairs={{0,1},{1,2},{2,3},{3,4},{4,5},{5,6},{6,7},{7,8},{8,9},{9,10},{10,1... | collective-permute-start | bytes 786440 | tf_op jit(solution)/shard_map/while/body/eval_jaxpr/ppermute | solution.py:13
  527.1 11.9 %collective-permute-start.3 = (bf16[128,1024]{1,0:T(8,128)(2,1)}, bf16[128,1024]{1,0:T(8,128)(2,1)S(1)}, u32[]{:S(2)}, u32[]{:S(2)}) collective-permute-start(bf16[128,1024]{1,0:T(8,128)(2,1)} %get-tuple-element.228), channel_id=1, source_target_pairs={{0,1},{1,2},{2,3},{3,4},{4,5},{5,6},{6,7},{7,8},{8,9},{9,10},{10,1... | collective-permute-start | bytes 786440 | tf_op jit(solution)/shard_map/ppermute | solution.py:13
  (1 other events, 5.8 us)
Sparse Core Ops, SparseCore 0:
  539.9 176.4 all-reduce.1
where the time goes:
time: 728 us; the launch traced here: 725 us
  waiting for transfers between devices  459 us (63%)
  starting transfers between devices  145 us (20%)
  matrix products  95.9 us (13%)
  between operations  14.1 us (2%)
  other arithmetic  7.82 us (1%)
    ppermute x62, waiting for transfers between devices, passed_along(): lax.ppermute(array, axis, [(i, (i + by) % peers) for i in range(peers)])  283 us
    psum x1, waiting for transfers between devices, body(): summed = lax.psum(finished.astype(jnp.bfloat16), 'dp').astype(jnp.float32)  176 us
    ppermute x62, starting transfers between devices, passed_along(): lax.ppermute(array, axis, [(i, (i + by) % peers) for i in range(peers)])  145 us
    dot_general x32, matrix products, visit(): lax.dot_general(out_grad, weight, (((1,), (1,)), ((), ())), preferred_ele...  57.1 us
    dot_general x32, matrix products, visit(): lax.dot_general(hidden_part, out_grad, (((0,), (0,)), ((), ())), preferre...  30.2 us
  transfers between devices with their start and end apart: 63, of which 63 were waited for; matrix products, arithmetic and copies ran while one was open for 3% of the time, Pallas kernels for 0%

commit v1 on v0

--- a/solution.py
+++ b/solution.py
@@ -86,7 +86,9 @@
     )
     finished = finish_partial(pass_grad(partial_value), own_term)
     out_total, grad_buffer = carried
-    summed = lax.psum(finished.astype(jnp.bfloat16), "dp").astype(jnp.float32)
+    summed = jnp.sum(lax.all_gather(finished.astype(jnp.bfloat16), "dp"), axis=0).astype(
+        jnp.float32
+    )
     token_count = row_count * cycle_size * lax.axis_size("dp")
     return (out_total.astype(jnp.bfloat16), grad_buffer, summed / math.sqrt(token_count))
 

time: 728 us -> 648 us (0.89)
  waiting for transfers between devices: 459 us -> 377 us
    psum x1 -> x0, waiting for transfers between devices: 176 us -> none  [body(): summed = lax.psum(finished.astype(jnp.bfloat16), 'dp').astype(jnp.float32)]
    all_gather x0 -> x1, waiting for transfers between devices: none -> 94.2 us  [body(): lax.all_gather(finished.astype(jnp.bfloat16), 'dp')]
where the time goes in v1:
time: 648 us; the launch traced here: 646 us
  waiting for transfers between devices  377 us (58%)
  starting transfers between devices  145 us (22%)
  matrix products  95.9 us (15%)
  between operations  14.1 us (2%)
  other arithmetic  9.99 us (2%)
    ppermute x62, waiting for transfers between devices, passed_along(): lax.ppermute(array, axis, [(i, (i + by) % peers) for i in range(peers)])  283 us
    ppermute x62, starting transfers between devices, passed_along(): lax.ppermute(array, axis, [(i, (i + by) % peers) for i in range(peers)])  145 us
    all_gather x1, waiting for transfers between devices, body(): lax.all_gather(finished.astype(jnp.bfloat16), 'dp')  94.2 us
    dot_general x32, matrix products, visit(): lax.dot_general(out_grad, weight, (((1,), (1,)), ((), ())), preferred_ele...  57.1 us
    dot_general x32, matrix products, visit(): lax.dot_general(hidden_part, out_grad, (((0,), (0,)), ((), ())), preferre...  30.2 us
  transfers between devices with their start and end apart: 63, of which 63 were waited for; matrix products, arithmetic and copies ran while one was open for 3% of the time, Pallas kernels for 0%

profile of v1, /device:TPU:1, one launch (start us, length us, event | category | flops | bytes accessed | tf_op | source)
XLA Modules:
  0.0 645.6 jit_solution(17437837454044028708)
XLA Ops:
  7.2 4.4 collective-permute-start.2
  11.6 4.5 fusion.14
  20.4 5.9 collective-permute-done.2
  28.4 498.7 %while.21 = (s32[]{:T(128)}, bf16[128,1024]{1,0:T(8,128)(2,1)S(1)}, bf16[128,1024]{1,0:T(8,128)(2,1)}, f32[192,1024]{1,0:T(8,128)S(1)}, bf16[192,4096]{1,0:T(8,1...) while((s32[]{:T(128)}, bf16[128,1024]{1,0:T(8,128)(2,1)S(1)}, ...), condition=%wide.region_1.2_spmd, body=%wide.region_0.1_spmd.sunk | while | flops 151633936 | bytes 6275492 | solution.py:84
  32.3 6.7 %collective-permute-done = bf16[128,1024]{1,0:T(8,128)(2,1)S(1)} collective-permute-done((bf16[128,1024]{1,0:T(8,128)(2,1)S(1)}, bf16[128,1024]{1,0:T(8,128)(2,1)S(1)}, u32[]{:S(2)}, u32[]{:S(2)}) %collective-permute-start) | collective-permute-done | bytes 262176 | tf_op jit(solution)/shard_map/while/body/eval_jaxpr/ppermute | solution.py:13
  39.3 5.3 collective-permute-done.1
  51.2 5.8 collective-permute-done
  57.3 5.3 collective-permute-done.1
  69.2 5.3 collective-permute-done
  74.9 4.8 collective-permute-done.1
  86.3 5.3 collective-permute-done
  91.9 3.9 collective-permute-done.1
  102.4 5.3 collective-permute-done
  108.1 3.0 collective-permute-done.1
  117.7 5.3 collective-permute-done
  123.3 2.5 collective-permute-done.1
  132.5 5.3 collective-permute-done
  138.1 2.5 collective-permute-done.1
  145.3 3.0 collective-permute-start.1
  148.3 4.2 collective-permute-done
  158.1 2.7 collective-permute-start
  160.9 4.0 collective-permute-start.1
  167.6 2.7 collective-permute-done.1
  173.1 3.9 collective-permute-start
  177.0 4.4 collective-permute-start.1
  183.0 3.4 collective-permute-done.1
  189.1 5.1 collective-permute-start
  194.2 4.0 collective-permute-start.1
  199.3 4.4 collective-permute-done.1
  206.4 4.5 collective-permute-start
  211.0 4.0 collective-permute-start.1
  215.9 4.5 collective-permute-done.1
  223.2 2.9 collective-permute-start
  226.1 4.0 collective-permute-start.1
  232.7 2.8 collective-permute-done.1
  240.2 4.0 collective-permute-start.1
  244.2 4.8 collective-permute-done
  258.5 8.2 %collective-permute-done = bf16[128,1024]{1,0:T(8,128)(2,1)S(1)} collective-permute-done((bf16[128,1024]{1,0:T(8,128)(2,1)S(1)}, bf16[128,1024]{1,0:T(8,128)(2,1)S(1)}, u32[]{:S(2)}, u32[]{:S(2)}) %collective-permute-start) | collective-permute-done | bytes 262176 | tf_op jit(solution)/shard_map/while/body/eval_jaxpr/ppermute | solution.py:13
  267.0 5.3 collective-permute-done.1
  278.9 7.3 %collective-permute-done = bf16[128,1024]{1,0:T(8,128)(2,1)S(1)} collective-permute-done((bf16[128,1024]{1,0:T(8,128)(2,1)S(1)}, bf16[128,1024]{1,0:T(8,128)(2,1)S(1)}, u32[]{:S(2)}, u32[]{:S(2)}) %collective-permute-start) | collective-permute-done | bytes 262176 | tf_op jit(solution)/shard_map/while/body/eval_jaxpr/ppermute | solution.py:13
  286.5 5.3 collective-permute-done.1
  298.5 6.4 collective-permute-done
  305.2 5.3 collective-permute-done.1
  317.1 5.3 collective-permute-done
  322.7 5.5 collective-permute-done.1
  334.8 5.3 collective-permute-done
  340.5 4.5 collective-permute-done.1
  351.6 5.3 collective-permute-done
  357.3 3.6 collective-permute-done.1
  367.5 5.3 collective-permute-done
  382.3 5.5 collective-permute-done
  397.2 5.3 collective-permute-done
  412.0 5.3 collective-permute-done
  426.7 5.3 collective-permute-done
  441.5 6.3 collective-permute-done
  457.5 7.1 %collective-permute-done = bf16[128,1024]{1,0:T(8,128)(2,1)S(1)} collective-permute-done((bf16[128,1024]{1,0:T(8,128)(2,1)S(1)}, bf16[128,1024]{1,0:T(8,128)(2,1)S(1)}, u32[]{:S(2)}, u32[]{:S(2)}) %collective-permute-start) | collective-permute-done | bytes 262176 | tf_op jit(solution)/shard_map/while/body/eval_jaxpr/ppermute | solution.py:13
  474.0 8.5 %collective-permute-done = bf16[128,1024]{1,0:T(8,128)(2,1)S(1)} collective-permute-done((bf16[128,1024]{1,0:T(8,128)(2,1)S(1)}, bf16[128,1024]{1,0:T(8,128)(2,1)S(1)}, u32[]{:S(2)}, u32[]{:S(2)}) %collective-permute-start) | collective-permute-done | bytes 262176 | tf_op jit(solution)/shard_map/while/body/eval_jaxpr/ppermute | solution.py:13
  491.9 8.5 %collective-permute-done = bf16[128,1024]{1,0:T(8,128)(2,1)S(1)} collective-permute-done((bf16[128,1024]{1,0:T(8,128)(2,1)S(1)}, bf16[128,1024]{1,0:T(8,128)(2,1)S(1)}, u32[]{:S(2)}, u32[]{:S(2)}) %collective-permute-start) | collective-permute-done | bytes 262176 | tf_op jit(solution)/shard_map/while/body/eval_jaxpr/ppermute | solution.py:13
  500.7 3.5 collective-permute-done.1
  510.9 8.3 %collective-permute-done = bf16[128,1024]{1,0:T(8,128)(2,1)S(1)} collective-permute-done((bf16[128,1024]{1,0:T(8,128)(2,1)S(1)}, bf16[128,1024]{1,0:T(8,128)(2,1)S(1)}, u32[]{:S(2)}, u32[]{:S(2)}) %collective-permute-start) | collective-permute-done | bytes 262176 | tf_op jit(solution)/shard_map/while/body/eval_jaxpr/ppermute | solution.py:13
  519.5 4.8 collective-permute-done.1
  529.2 9.8 %collective-permute-done.3 = bf16[128,1024]{1,0:T(8,128)(2,1)S(1)} collective-permute-done((bf16[128,1024]{1,0:T(8,128)(2,1)}, bf16[128,1024]{1,0:T(8,128)(2,1)S(1)}, u32[]{:S(2)}, u32[]{:S(2)}) %collective-permute-start.3) | collective-permute-done | bytes 262176 | tf_op jit(solution)/shard_map/ppermute | solution.py:13
  540.6 94.2 %all-gather.3.cloned.1.call-done = bf16[2048,1024]{1,0:T(8,128)(2,1)} async-done(((bf16[128,1024]{1,0:T(8,128)(2,1)}), bf16[2048,1024]{1,0:T(8,128)(2,1)}) %all-gather.3.cloned.1.call-update) | async-done | bytes 4194320 | tf_op jit(solution)/shard_map/all_gather | solution.py:89
  634.8 3.1 reduce_sum.12
  (200 shorter events, 226.7 us)
Async XLA Ops:
  7.2 627.6 %all-gather.3.cloned.1.call-start = ((), (), s32[]{:S(2)}) async-start(), calls=%async_computation | async-start | bytes 4456448 | tf_op jit(solution)/shard_map/all_gather | solution.py:89
  7.2 19.1 %collective-permute-start.2 = (bf16[128,1024]{1,0:T(8,128)(2,1)}, bf16[128,1024]{1,0:T(8,128)(2,1)S(1)}, u32[]{:S(2)}, u32[]{:S(2)}) collective-permute-start(bf16[128,1024]{1,0:T(8,128)(2,1)} %param.7), channel_id=1, source_target_pairs={{0,1},{1,2},{2,3},{3,4},{4,5},{5,6},{6,7},{7,8},{8,9},{9,10},{10,1... | collective-permute-start | bytes 786440 | tf_op jit(solution)/shard_map/ppermute | solution.py:13
  11.6 5.8 copy-start
  28.4 10.6 %collective-permute-start = (bf16[128,1024]{1,0:T(8,128)(2,1)S(1)}, bf16[128,1024]{1,0:T(8,128)(2,1)S(1)}, u32[]{:S(2)}, u32[]{:S(2)}) collective-permute-start(bf16[128,1024]{1,0:T(8,128)(2,1)S(1)} %get-tuple-element.321), channel_id=1, source_target_pairs={{0,1},{1,2},{2,3},{3,4},{4,5},{5,6},{6,7},{7,8},{8,9},{9,10},{10,1... | collective-permute-start | bytes 786440 | tf_op jit(solution)/shard_map/while/body/eval_jaxpr/ppermute | solution.py:13
  30.3 14.3 %collective-permute-start.1 = (bf16[128,1024]{1,0:T(8,128)(2,1)}, bf16[128,1024]{1,0:T(8,128)(2,1)S(1)}, u32[]{:S(2)}, u32[]{:S(2)}) collective-permute-start(bf16[128,1024]{1,0:T(8,128)(2,1)} %get-tuple-element.322), channel_id=1, source_target_pairs={{0,1},{1,2},{2,3},{3,4},{4,5},{5,6},{6,7},{7,8},{8,9},{9,10},{10,1... | collective-permute-start | bytes 786440 | tf_op jit(solution)/shard_map/while/body/eval_jaxpr/ppermute | solution.py:13
  47.3 9.6 %collective-permute-start = (bf16[128,1024]{1,0:T(8,128)(2,1)S(1)}, bf16[128,1024]{1,0:T(8,128)(2,1)S(1)}, u32[]{:S(2)}, u32[]{:S(2)}) collective-permute-start(bf16[128,1024]{1,0:T(8,128)(2,1)S(1)} %get-tuple-element.321), channel_id=1, source_target_pairs={{0,1},{1,2},{2,3},{3,4},{4,5},{5,6},{6,7},{7,8},{8,9},{9,10},{10,1... | collective-permute-start | bytes 786440 | tf_op jit(solution)/shard_map/while/body/eval_jaxpr/ppermute | solution.py:13
  49.3 13.3 %collective-permute-start.1 = (bf16[128,1024]{1,0:T(8,128)(2,1)}, bf16[128,1024]{1,0:T(8,128)(2,1)S(1)}, u32[]{:S(2)}, u32[]{:S(2)}) collective-permute-start(bf16[128,1024]{1,0:T(8,128)(2,1)} %get-tuple-element.322), channel_id=1, source_target_pairs={{0,1},{1,2},{2,3},{3,4},{4,5},{5,6},{6,7},{7,8},{8,9},{9,10},{10,1... | collective-permute-start | bytes 786440 | tf_op jit(solution)/shard_map/while/body/eval_jaxpr/ppermute | solution.py:13
  65.3 9.2 %collective-permute-start = (bf16[128,1024]{1,0:T(8,128)(2,1)S(1)}, bf16[128,1024]{1,0:T(8,128)(2,1)S(1)}, u32[]{:S(2)}, u32[]{:S(2)}) collective-permute-start(bf16[128,1024]{1,0:T(8,128)(2,1)S(1)} %get-tuple-element.321), channel_id=1, source_target_pairs={{0,1},{1,2},{2,3},{3,4},{4,5},{5,6},{6,7},{7,8},{8,9},{9,10},{10,1... | collective-permute-start | bytes 786440 | tf_op jit(solution)/shard_map/while/body/eval_jaxpr/ppermute | solution.py:13
  67.3 12.4 %collective-permute-start.1 = (bf16[128,1024]{1,0:T(8,128)(2,1)}, bf16[128,1024]{1,0:T(8,128)(2,1)S(1)}, u32[]{:S(2)}, u32[]{:S(2)}) collective-permute-start(bf16[128,1024]{1,0:T(8,128)(2,1)} %get-tuple-element.322), channel_id=1, source_target_pairs={{0,1},{1,2},{2,3},{3,4},{4,5},{5,6},{6,7},{7,8},{8,9},{9,10},{10,1... | collective-permute-start | bytes 786440 | tf_op jit(solution)/shard_map/while/body/eval_jaxpr/ppermute | solution.py:13
  82.4 9.2 %collective-permute-start = (bf16[128,1024]{1,0:T(8,128)(2,1)S(1)}, bf16[128,1024]{1,0:T(8,128)(2,1)S(1)}, u32[]{:S(2)}, u32[]{:S(2)}) collective-permute-start(bf16[128,1024]{1,0:T(8,128)(2,1)S(1)} %get-tuple-element.321), channel_id=1, source_target_pairs={{0,1},{1,2},{2,3},{3,4},{4,5},{5,6},{6,7},{7,8},{8,9},{9,10},{10,1... | collective-permute-start | bytes 786440 | tf_op jit(solution)/shard_map/while/body/eval_jaxpr/ppermute | solution.py:13
  84.3 11.5 %collective-permute-start.1 = (bf16[128,1024]{1,0:T(8,128)(2,1)}, bf16[128,1024]{1,0:T(8,128)(2,1)S(1)}, u32[]{:S(2)}, u32[]{:S(2)}) collective-permute-start(bf16[128,1024]{1,0:T(8,128)(2,1)} %get-tuple-element.322), channel_id=1, source_target_pairs={{0,1},{1,2},{2,3},{3,4},{4,5},{5,6},{6,7},{7,8},{8,9},{9,10},{10,1... | collective-permute-start | bytes 786440 | tf_op jit(solution)/shard_map/while/body/eval_jaxpr/ppermute | solution.py:13
  98.6 9.2 %collective-permute-start = (bf16[128,1024]{1,0:T(8,128)(2,1)S(1)}, bf16[128,1024]{1,0:T(8,128)(2,1)S(1)}, u32[]{:S(2)}, u32[]{:S(2)}) collective-permute-start(bf16[128,1024]{1,0:T(8,128)(2,1)S(1)} %get-tuple-element.321), channel_id=1, source_target_pairs={{0,1},{1,2},{2,3},{3,4},{4,5},{5,6},{6,7},{7,8},{8,9},{9,10},{10,1... | collective-permute-start | bytes 786440 | tf_op jit(solution)/shard_map/while/body/eval_jaxpr/ppermute | solution.py:13
  100.5 10.6 %collective-permute-start.1 = (bf16[128,1024]{1,0:T(8,128)(2,1)}, bf16[128,1024]{1,0:T(8,128)(2,1)S(1)}, u32[]{:S(2)}, u32[]{:S(2)}) collective-permute-start(bf16[128,1024]{1,0:T(8,128)(2,1)} %get-tuple-element.322), channel_id=1, source_target_pairs={{0,1},{1,2},{2,3},{3,4},{4,5},{5,6},{6,7},{7,8},{8,9},{9,10},{10,1... | collective-permute-start | bytes 786440 | tf_op jit(solution)/shard_map/while/body/eval_jaxpr/ppermute | solution.py:13
  113.8 9.2 %collective-permute-start = (bf16[128,1024]{1,0:T(8,128)(2,1)S(1)}, bf16[128,1024]{1,0:T(8,128)(2,1)S(1)}, u32[]{:S(2)}, u32[]{:S(2)}) collective-permute-start(bf16[128,1024]{1,0:T(8,128)(2,1)S(1)} %get-tuple-element.321), channel_id=1, source_target_pairs={{0,1},{1,2},{2,3},{3,4},{4,5},{5,6},{6,7},{7,8},{8,9},{9,10},{10,1... | collective-permute-start | bytes 786440 | tf_op jit(solution)/shard_map/while/body/eval_jaxpr/ppermute | solution.py:13
  115.7 10.1 %collective-permute-start.1 = (bf16[128,1024]{1,0:T(8,128)(2,1)}, bf16[128,1024]{1,0:T(8,128)(2,1)S(1)}, u32[]{:S(2)}, u32[]{:S(2)}) collective-permute-start(bf16[128,1024]{1,0:T(8,128)(2,1)} %get-tuple-element.322), channel_id=1, source_target_pairs={{0,1},{1,2},{2,3},{3,4},{4,5},{5,6},{6,7},{7,8},{8,9},{9,10},{10,1... | collective-permute-start | bytes 786440 | tf_op jit(solution)/shard_map/while/body/eval_jaxpr/ppermute | solution.py:13
  128.6 9.2 %collective-permute-start = (bf16[128,1024]{1,0:T(8,128)(2,1)S(1)}, bf16[128,1024]{1,0:T(8,128)(2,1)S(1)}, u32[]{:S(2)}, u32[]{:S(2)}) collective-permute-start(bf16[128,1024]{1,0:T(8,128)(2,1)S(1)} %get-tuple-element.321), channel_id=1, source_target_pairs={{0,1},{1,2},{2,3},{3,4},{4,5},{5,6},{6,7},{7,8},{8,9},{9,10},{10,1... | collective-permute-start | bytes 786440 | tf_op jit(solution)/shard_map/while/body/eval_jaxpr/ppermute | solution.py:13
  130.5 10.1 %collective-permute-start.1 = (bf16[128,1024]{1,0:T(8,128)(2,1)}, bf16[128,1024]{1,0:T(8,128)(2,1)S(1)}, u32[]{:S(2)}, u32[]{:S(2)}) collective-permute-start(bf16[128,1024]{1,0:T(8,128)(2,1)} %get-tuple-element.322), channel_id=1, source_target_pairs={{0,1},{1,2},{2,3},{3,4},{4,5},{5,6},{6,7},{7,8},{8,9},{9,10},{10,1... | collective-permute-start | bytes 786440 | tf_op jit(solution)/shard_map/while/body/eval_jaxpr/ppermute | solution.py:13
  143.4 9.2 %collective-permute-start = (bf16[128,1024]{1,0:T(8,128)(2,1)S(1)}, bf16[128,1024]{1,0:T(8,128)(2,1)S(1)}, u32[]{:S(2)}, u32[]{:S(2)}) collective-permute-start(bf16[128,1024]{1,0:T(8,128)(2,1)S(1)} %get-tuple-element.321), channel_id=1, source_target_pairs={{0,1},{1,2},{2,3},{3,4},{4,5},{5,6},{6,7},{7,8},{8,9},{9,10},{10,1... | collective-permute-start | bytes 786440 | tf_op jit(solution)/shard_map/while/body/eval_jaxpr/ppermute | solution.py:13
  145.3 10.1 %collective-permute-start.1 = (bf16[128,1024]{1,0:T(8,128)(2,1)}, bf16[128,1024]{1,0:T(8,128)(2,1)S(1)}, u32[]{:S(2)}, u32[]{:S(2)}) collective-permute-start(bf16[128,1024]{1,0:T(8,128)(2,1)} %get-tuple-element.322), channel_id=1, source_target_pairs={{0,1},{1,2},{2,3},{3,4},{4,5},{5,6},{6,7},{7,8},{8,9},{9,10},{10,1... | collective-permute-start | bytes 786440 | tf_op jit(solution)/shard_map/while/body/eval_jaxpr/ppermute | solution.py:13
  158.1 9.2 %collective-permute-start = (bf16[128,1024]{1,0:T(8,128)(2,1)S(1)}, bf16[128,1024]{1,0:T(8,128)(2,1)S(1)}, u32[]{:S(2)}, u32[]{:S(2)}) collective-permute-start(bf16[128,1024]{1,0:T(8,128)(2,1)S(1)} %get-tuple-element.321), channel_id=1, source_target_pairs={{0,1},{1,2},{2,3},{3,4},{4,5},{5,6},{6,7},{7,8},{8,9},{9,10},{10,1... | collective-permute-start | bytes 786440 | tf_op jit(solution)/shard_map/while/body/eval_jaxpr/ppermute | solution.py:13
  160.9 9.4 %collective-permute-start.1 = (bf16[128,1024]{1,0:T(8,128)(2,1)}, bf16[128,1024]{1,0:T(8,128)(2,1)S(1)}, u32[]{:S(2)}, u32[]{:S(2)}) collective-permute-start(bf16[128,1024]{1,0:T(8,128)(2,1)} %get-tuple-element.322), channel_id=1, source_target_pairs={{0,1},{1,2},{2,3},{3,4},{4,5},{5,6},{6,7},{7,8},{8,9},{9,10},{10,1... | collective-permute-start | bytes 786440 | tf_op jit(solution)/shard_map/while/body/eval_jaxpr/ppermute | solution.py:13
  173.1 9.6 %collective-permute-start = (bf16[128,1024]{1,0:T(8,128)(2,1)S(1)}, bf16[128,1024]{1,0:T(8,128)(2,1)S(1)}, u32[]{:S(2)}, u32[]{:S(2)}) collective-permute-start(bf16[128,1024]{1,0:T(8,128)(2,1)S(1)} %get-tuple-element.321), channel_id=1, source_target_pairs={{0,1},{1,2},{2,3},{3,4},{4,5},{5,6},{6,7},{7,8},{8,9},{9,10},{10,1... | collective-permute-start | bytes 786440 | tf_op jit(solution)/shard_map/while/body/eval_jaxpr/ppermute | solution.py:13
  177.0 9.4 %collective-permute-start.1 = (bf16[128,1024]{1,0:T(8,128)(2,1)}, bf16[128,1024]{1,0:T(8,128)(2,1)S(1)}, u32[]{:S(2)}, u32[]{:S(2)}) collective-permute-start(bf16[128,1024]{1,0:T(8,128)(2,1)} %get-tuple-element.322), channel_id=1, source_target_pairs={{0,1},{1,2},{2,3},{3,4},{4,5},{5,6},{6,7},{7,8},{8,9},{9,10},{10,1... | collective-permute-start | bytes 786440 | tf_op jit(solution)/shard_map/while/body/eval_jaxpr/ppermute | solution.py:13
  189.1 9.9 %collective-permute-start = (bf16[128,1024]{1,0:T(8,128)(2,1)S(1)}, bf16[128,1024]{1,0:T(8,128)(2,1)S(1)}, u32[]{:S(2)}, u32[]{:S(2)}) collective-permute-start(bf16[128,1024]{1,0:T(8,128)(2,1)S(1)} %get-tuple-element.321), channel_id=1, source_target_pairs={{0,1},{1,2},{2,3},{3,4},{4,5},{5,6},{6,7},{7,8},{8,9},{9,10},{10,1... | collective-permute-start | bytes 786440 | tf_op jit(solution)/shard_map/while/body/eval_jaxpr/ppermute | solution.py:13
  194.2 9.4 %collective-permute-start.1 = (bf16[128,1024]{1,0:T(8,128)(2,1)}, bf16[128,1024]{1,0:T(8,128)(2,1)S(1)}, u32[]{:S(2)}, u32[]{:S(2)}) collective-permute-start(bf16[128,1024]{1,0:T(8,128)(2,1)} %get-tuple-element.322), channel_id=1, source_target_pairs={{0,1},{1,2},{2,3},{3,4},{4,5},{5,6},{6,7},{7,8},{8,9},{9,10},{10,1... | collective-permute-start | bytes 786440 | tf_op jit(solution)/shard_map/while/body/eval_jaxpr/ppermute | solution.py:13
  206.4 9.2 %collective-permute-start = (bf16[128,1024]{1,0:T(8,128)(2,1)S(1)}, bf16[128,1024]{1,0:T(8,128)(2,1)S(1)}, u32[]{:S(2)}, u32[]{:S(2)}) collective-permute-start(bf16[128,1024]{1,0:T(8,128)(2,1)S(1)} %get-tuple-element.321), channel_id=1, source_target_pairs={{0,1},{1,2},{2,3},{3,4},{4,5},{5,6},{6,7},{7,8},{8,9},{9,10},{10,1... | collective-permute-start | bytes 786440 | tf_op jit(solution)/shard_map/while/body/eval_jaxpr/ppermute | solution.py:13
  211.0 9.4 %collective-permute-start.1 = (bf16[128,1024]{1,0:T(8,128)(2,1)}, bf16[128,1024]{1,0:T(8,128)(2,1)S(1)}, u32[]{:S(2)}, u32[]{:S(2)}) collective-permute-start(bf16[128,1024]{1,0:T(8,128)(2,1)} %get-tuple-element.322), channel_id=1, source_target_pairs={{0,1},{1,2},{2,3},{3,4},{4,5},{5,6},{6,7},{7,8},{8,9},{9,10},{10,1... | collective-permute-start | bytes 786440 | tf_op jit(solution)/shard_map/while/body/eval_jaxpr/ppermute | solution.py:13
  223.2 9.2 %collective-permute-start = (bf16[128,1024]{1,0:T(8,128)(2,1)S(1)}, bf16[128,1024]{1,0:T(8,128)(2,1)S(1)}, u32[]{:S(2)}, u32[]{:S(2)}) collective-permute-start(bf16[128,1024]{1,0:T(8,128)(2,1)S(1)} %get-tuple-element.321), channel_id=1, source_target_pairs={{0,1},{1,2},{2,3},{3,4},{4,5},{5,6},{6,7},{7,8},{8,9},{9,10},{10,1... | collective-permute-start | bytes 786440 | tf_op jit(solution)/shard_map/while/body/eval_jaxpr/ppermute | solution.py:13
  226.1 9.4 %collective-permute-start.1 = (bf16[128,1024]{1,0:T(8,128)(2,1)}, bf16[128,1024]{1,0:T(8,128)(2,1)S(1)}, u32[]{:S(2)}, u32[]{:S(2)}) collective-permute-start(bf16[128,1024]{1,0:T(8,128)(2,1)} %get-tuple-element.322), channel_id=1, source_target_pairs={{0,1},{1,2},{2,3},{3,4},{4,5},{5,6},{6,7},{7,8},{8,9},{9,10},{10,1... | collective-permute-start | bytes 786440 | tf_op jit(solution)/shard_map/while/body/eval_jaxpr/ppermute | solution.py:13
  238.2 10.8 %collective-permute-start = (bf16[128,1024]{1,0:T(8,128)(2,1)S(1)}, bf16[128,1024]{1,0:T(8,128)(2,1)S(1)}, u32[]{:S(2)}, u32[]{:S(2)}) collective-permute-start(bf16[128,1024]{1,0:T(8,128)(2,1)S(1)} %get-tuple-element.321), channel_id=1, source_target_pairs={{0,1},{1,2},{2,3},{3,4},{4,5},{5,6},{6,7},{7,8},{8,9},{9,10},{10,1... | collective-permute-start | bytes 786440 | tf_op jit(solution)/shard_map/while/body/eval_jaxpr/ppermute | solution.py:13
  240.2 11.6 %collective-permute-start.1 = (bf16[128,1024]{1,0:T(8,128)(2,1)}, bf16[128,1024]{1,0:T(8,128)(2,1)S(1)}, u32[]{:S(2)}, u32[]{:S(2)}) collective-permute-start(bf16[128,1024]{1,0:T(8,128)(2,1)} %get-tuple-element.322), channel_id=1, source_target_pairs={{0,1},{1,2},{2,3},{3,4},{4,5},{5,6},{6,7},{7,8},{8,9},{9,10},{10,1... | collective-permute-start | bytes 786440 | tf_op jit(solution)/shard_map/while/body/eval_jaxpr/ppermute | solution.py:13
  254.6 12.1 %collective-permute-start = (bf16[128,1024]{1,0:T(8,128)(2,1)S(1)}, bf16[128,1024]{1,0:T(8,128)(2,1)S(1)}, u32[]{:S(2)}, u32[]{:S(2)}) collective-permute-start(bf16[128,1024]{1,0:T(8,128)(2,1)S(1)} %get-tuple-element.321), channel_id=1, source_target_pairs={{0,1},{1,2},{2,3},{3,4},{4,5},{5,6},{6,7},{7,8},{8,9},{9,10},{10,1... | collective-permute-start | bytes 786440 | tf_op jit(solution)/shard_map/while/body/eval_jaxpr/ppermute | solution.py:13
  256.5 15.8 %collective-permute-start.1 = (bf16[128,1024]{1,0:T(8,128)(2,1)}, bf16[128,1024]{1,0:T(8,128)(2,1)S(1)}, u32[]{:S(2)}, u32[]{:S(2)}) collective-permute-start(bf16[128,1024]{1,0:T(8,128)(2,1)} %get-tuple-element.322), channel_id=1, source_target_pairs={{0,1},{1,2},{2,3},{3,4},{4,5},{5,6},{6,7},{7,8},{8,9},{9,10},{10,1... | collective-permute-start | bytes 786440 | tf_op jit(solution)/shard_map/while/body/eval_jaxpr/ppermute | solution.py:13
  275.0 11.2 %collective-permute-start = (bf16[128,1024]{1,0:T(8,128)(2,1)S(1)}, bf16[128,1024]{1,0:T(8,128)(2,1)S(1)}, u32[]{:S(2)}, u32[]{:S(2)}) collective-permute-start(bf16[128,1024]{1,0:T(8,128)(2,1)S(1)} %get-tuple-element.321), channel_id=1, source_target_pairs={{0,1},{1,2},{2,3},{3,4},{4,5},{5,6},{6,7},{7,8},{8,9},{9,10},{10,1... | collective-permute-start | bytes 786440 | tf_op jit(solution)/shard_map/while/body/eval_jaxpr/ppermute | solution.py:13
  276.9 14.9 %collective-permute-start.1 = (bf16[128,1024]{1,0:T(8,128)(2,1)}, bf16[128,1024]{1,0:T(8,128)(2,1)S(1)}, u32[]{:S(2)}, u32[]{:S(2)}) collective-permute-start(bf16[128,1024]{1,0:T(8,128)(2,1)} %get-tuple-element.322), channel_id=1, source_target_pairs={{0,1},{1,2},{2,3},{3,4},{4,5},{5,6},{6,7},{7,8},{8,9},{9,10},{10,1... | collective-permute-start | bytes 786440 | tf_op jit(solution)/shard_map/while/body/eval_jaxpr/ppermute | solution.py:13
  294.6 10.3 %collective-permute-start = (bf16[128,1024]{1,0:T(8,128)(2,1)S(1)}, bf16[128,1024]{1,0:T(8,128)(2,1)S(1)}, u32[]{:S(2)}, u32[]{:S(2)}) collective-permute-start(bf16[128,1024]{1,0:T(8,128)(2,1)S(1)} %get-tuple-element.321), channel_id=1, source_target_pairs={{0,1},{1,2},{2,3},{3,4},{4,5},{5,6},{6,7},{7,8},{8,9},{9,10},{10,1... | collective-permute-start | bytes 786440 | tf_op jit(solution)/shard_map/while/body/eval_jaxpr/ppermute | solution.py:13
  296.5 14.0 %collective-permute-start.1 = (bf16[128,1024]{1,0:T(8,128)(2,1)}, bf16[128,1024]{1,0:T(8,128)(2,1)S(1)}, u32[]{:S(2)}, u32[]{:S(2)}) collective-permute-start(bf16[128,1024]{1,0:T(8,128)(2,1)} %get-tuple-element.322), channel_id=1, source_target_pairs={{0,1},{1,2},{2,3},{3,4},{4,5},{5,6},{6,7},{7,8},{8,9},{9,10},{10,1... | collective-permute-start | bytes 786440 | tf_op jit(solution)/shard_map/while/body/eval_jaxpr/ppermute | solution.py:13
  313.2 9.2 %collective-permute-start = (bf16[128,1024]{1,0:T(8,128)(2,1)S(1)}, bf16[128,1024]{1,0:T(8,128)(2,1)S(1)}, u32[]{:S(2)}, u32[]{:S(2)}) collective-permute-start(bf16[128,1024]{1,0:T(8,128)(2,1)S(1)} %get-tuple-element.321), channel_id=1, source_target_pairs={{0,1},{1,2},{2,3},{3,4},{4,5},{5,6},{6,7},{7,8},{8,9},{9,10},{10,1... | collective-permute-start | bytes 786440 | tf_op jit(solution)/shard_map/while/body/eval_jaxpr/ppermute | solution.py:13
  315.1 13.1 %collective-permute-start.1 = (bf16[128,1024]{1,0:T(8,128)(2,1)}, bf16[128,1024]{1,0:T(8,128)(2,1)S(1)}, u32[]{:S(2)}, u32[]{:S(2)}) collective-permute-start(bf16[128,1024]{1,0:T(8,128)(2,1)} %get-tuple-element.322), channel_id=1, source_target_pairs={{0,1},{1,2},{2,3},{3,4},{4,5},{5,6},{6,7},{7,8},{8,9},{9,10},{10,1... | collective-permute-start | bytes 786440 | tf_op jit(solution)/shard_map/while/body/eval_jaxpr/ppermute | solution.py:13
  330.9 9.2 %collective-permute-start = (bf16[128,1024]{1,0:T(8,128)(2,1)S(1)}, bf16[128,1024]{1,0:T(8,128)(2,1)S(1)}, u32[]{:S(2)}, u32[]{:S(2)}) collective-permute-start(bf16[128,1024]{1,0:T(8,128)(2,1)S(1)} %get-tuple-element.321), channel_id=1, source_target_pairs={{0,1},{1,2},{2,3},{3,4},{4,5},{5,6},{6,7},{7,8},{8,9},{9,10},{10,1... | collective-permute-start | bytes 786440 | tf_op jit(solution)/shard_map/while/body/eval_jaxpr/ppermute | solution.py:13
  332.9 12.1 %collective-permute-start.1 = (bf16[128,1024]{1,0:T(8,128)(2,1)}, bf16[128,1024]{1,0:T(8,128)(2,1)S(1)}, u32[]{:S(2)}, u32[]{:S(2)}) collective-permute-start(bf16[128,1024]{1,0:T(8,128)(2,1)} %get-tuple-element.322), channel_id=1, source_target_pairs={{0,1},{1,2},{2,3},{3,4},{4,5},{5,6},{6,7},{7,8},{8,9},{9,10},{10,1... | collective-permute-start | bytes 786440 | tf_op jit(solution)/shard_map/while/body/eval_jaxpr/ppermute | solution.py:13
  347.7 9.2 %collective-permute-start = (bf16[128,1024]{1,0:T(8,128)(2,1)S(1)}, bf16[128,1024]{1,0:T(8,128)(2,1)S(1)}, u32[]{:S(2)}, u32[]{:S(2)}) collective-permute-start(bf16[128,1024]{1,0:T(8,128)(2,1)S(1)} %get-tuple-element.321), channel_id=1, source_target_pairs={{0,1},{1,2},{2,3},{3,4},{4,5},{5,6},{6,7},{7,8},{8,9},{9,10},{10,1... | collective-permute-start | bytes 786440 | tf_op jit(solution)/shard_map/while/body/eval_jaxpr/ppermute | solution.py:13
  349.7 11.2 %collective-permute-start.1 = (bf16[128,1024]{1,0:T(8,128)(2,1)}, bf16[128,1024]{1,0:T(8,128)(2,1)S(1)}, u32[]{:S(2)}, u32[]{:S(2)}) collective-permute-start(bf16[128,1024]{1,0:T(8,128)(2,1)} %get-tuple-element.322), channel_id=1, source_target_pairs={{0,1},{1,2},{2,3},{3,4},{4,5},{5,6},{6,7},{7,8},{8,9},{9,10},{10,1... | collective-permute-start | bytes 786440 | tf_op jit(solution)/shard_map/while/body/eval_jaxpr/ppermute | solution.py:13
  363.6 9.2 %collective-permute-start = (bf16[128,1024]{1,0:T(8,128)(2,1)S(1)}, bf16[128,1024]{1,0:T(8,128)(2,1)S(1)}, u32[]{:S(2)}, u32[]{:S(2)}) collective-permute-start(bf16[128,1024]{1,0:T(8,128)(2,1)S(1)} %get-tuple-element.321), channel_id=1, source_target_pairs={{0,1},{1,2},{2,3},{3,4},{4,5},{5,6},{6,7},{7,8},{8,9},{9,10},{10,1... | collective-permute-start | bytes 786440 | tf_op jit(solution)/shard_map/while/body/eval_jaxpr/ppermute | solution.py:13
  365.5 10.1 %collective-permute-start.1 = (bf16[128,1024]{1,0:T(8,128)(2,1)}, bf16[128,1024]{1,0:T(8,128)(2,1)S(1)}, u32[]{:S(2)}, u32[]{:S(2)}) collective-permute-start(bf16[128,1024]{1,0:T(8,128)(2,1)} %get-tuple-element.322), channel_id=1, source_target_pairs={{0,1},{1,2},{2,3},{3,4},{4,5},{5,6},{6,7},{7,8},{8,9},{9,10},{10,1... | collective-permute-start | bytes 786440 | tf_op jit(solution)/shard_map/while/body/eval_jaxpr/ppermute | solution.py:13
  378.4 9.4 %collective-permute-start = (bf16[128,1024]{1,0:T(8,128)(2,1)S(1)}, bf16[128,1024]{1,0:T(8,128)(2,1)S(1)}, u32[]{:S(2)}, u32[]{:S(2)}) collective-permute-start(bf16[128,1024]{1,0:T(8,128)(2,1)S(1)} %get-tuple-element.321), channel_id=1, source_target_pairs={{0,1},{1,2},{2,3},{3,4},{4,5},{5,6},{6,7},{7,8},{8,9},{9,10},{10,1... | collective-permute-start | bytes 786440 | tf_op jit(solution)/shard_map/while/body/eval_jaxpr/ppermute | solution.py:13
  380.3 10.3 %collective-permute-start.1 = (bf16[128,1024]{1,0:T(8,128)(2,1)}, bf16[128,1024]{1,0:T(8,128)(2,1)S(1)}, u32[]{:S(2)}, u32[]{:S(2)}) collective-permute-start(bf16[128,1024]{1,0:T(8,128)(2,1)} %get-tuple-element.322), channel_id=1, source_target_pairs={{0,1},{1,2},{2,3},{3,4},{4,5},{5,6},{6,7},{7,8},{8,9},{9,10},{10,1... | collective-permute-start | bytes 786440 | tf_op jit(solution)/shard_map/while/body/eval_jaxpr/ppermute | solution.py:13
  393.3 9.2 %collective-permute-start = (bf16[128,1024]{1,0:T(8,128)(2,1)S(1)}, bf16[128,1024]{1,0:T(8,128)(2,1)S(1)}, u32[]{:S(2)}, u32[]{:S(2)}) collective-permute-start(bf16[128,1024]{1,0:T(8,128)(2,1)S(1)} %get-tuple-element.321), channel_id=1, source_target_pairs={{0,1},{1,2},{2,3},{3,4},{4,5},{5,6},{6,7},{7,8},{8,9},{9,10},{10,1... | collective-permute-start | bytes 786440 | tf_op jit(solution)/shard_map/while/body/eval_jaxpr/ppermute | solution.py:13
  395.2 10.1 %collective-permute-start.1 = (bf16[128,1024]{1,0:T(8,128)(2,1)}, bf16[128,1024]{1,0:T(8,128)(2,1)S(1)}, u32[]{:S(2)}, u32[]{:S(2)}) collective-permute-start(bf16[128,1024]{1,0:T(8,128)(2,1)} %get-tuple-element.322), channel_id=1, source_target_pairs={{0,1},{1,2},{2,3},{3,4},{4,5},{5,6},{6,7},{7,8},{8,9},{9,10},{10,1... | collective-permute-start | bytes 786440 | tf_op jit(solution)/shard_map/while/body/eval_jaxpr/ppermute | solution.py:13
  408.1 9.2 %collective-permute-start = (bf16[128,1024]{1,0:T(8,128)(2,1)S(1)}, bf16[128,1024]{1,0:T(8,128)(2,1)S(1)}, u32[]{:S(2)}, u32[]{:S(2)}) collective-permute-start(bf16[128,1024]{1,0:T(8,128)(2,1)S(1)} %get-tuple-element.321), channel_id=1, source_target_pairs={{0,1},{1,2},{2,3},{3,4},{4,5},{5,6},{6,7},{7,8},{8,9},{9,10},{10,1... | collective-permute-start | bytes 786440 | tf_op jit(solution)/shard_map/while/body/eval_jaxpr/ppermute | solution.py:13
  410.0 10.1 %collective-permute-start.1 = (bf16[128,1024]{1,0:T(8,128)(2,1)}, bf16[128,1024]{1,0:T(8,128)(2,1)S(1)}, u32[]{:S(2)}, u32[]{:S(2)}) collective-permute-start(bf16[128,1024]{1,0:T(8,128)(2,1)} %get-tuple-element.322), channel_id=1, source_target_pairs={{0,1},{1,2},{2,3},{3,4},{4,5},{5,6},{6,7},{7,8},{8,9},{9,10},{10,1... | collective-permute-start | bytes 786440 | tf_op jit(solution)/shard_map/while/body/eval_jaxpr/ppermute | solution.py:13
  422.9 9.2 %collective-permute-start = (bf16[128,1024]{1,0:T(8,128)(2,1)S(1)}, bf16[128,1024]{1,0:T(8,128)(2,1)S(1)}, u32[]{:S(2)}, u32[]{:S(2)}) collective-permute-start(bf16[128,1024]{1,0:T(8,128)(2,1)S(1)} %get-tuple-element.321), channel_id=1, source_target_pairs={{0,1},{1,2},{2,3},{3,4},{4,5},{5,6},{6,7},{7,8},{8,9},{9,10},{10,1... | collective-permute-start | bytes 786440 | tf_op jit(solution)/shard_map/while/body/eval_jaxpr/ppermute | solution.py:13
  424.8 10.1 %collective-permute-start.1 = (bf16[128,1024]{1,0:T(8,128)(2,1)}, bf16[128,1024]{1,0:T(8,128)(2,1)S(1)}, u32[]{:S(2)}, u32[]{:S(2)}) collective-permute-start(bf16[128,1024]{1,0:T(8,128)(2,1)} %get-tuple-element.322), channel_id=1, source_target_pairs={{0,1},{1,2},{2,3},{3,4},{4,5},{5,6},{6,7},{7,8},{8,9},{9,10},{10,1... | collective-permute-start | bytes 786440 | tf_op jit(solution)/shard_map/while/body/eval_jaxpr/ppermute | solution.py:13
  437.6 10.2 %collective-permute-start = (bf16[128,1024]{1,0:T(8,128)(2,1)S(1)}, bf16[128,1024]{1,0:T(8,128)(2,1)S(1)}, u32[]{:S(2)}, u32[]{:S(2)}) collective-permute-start(bf16[128,1024]{1,0:T(8,128)(2,1)S(1)} %get-tuple-element.321), channel_id=1, source_target_pairs={{0,1},{1,2},{2,3},{3,4},{4,5},{5,6},{6,7},{7,8},{8,9},{9,10},{10,1... | collective-permute-start | bytes 786440 | tf_op jit(solution)/shard_map/while/body/eval_jaxpr/ppermute | solution.py:13
  439.5 11.1 %collective-permute-start.1 = (bf16[128,1024]{1,0:T(8,128)(2,1)}, bf16[128,1024]{1,0:T(8,128)(2,1)S(1)}, u32[]{:S(2)}, u32[]{:S(2)}) collective-permute-start(bf16[128,1024]{1,0:T(8,128)(2,1)} %get-tuple-element.322), channel_id=1, source_target_pairs={{0,1},{1,2},{2,3},{3,4},{4,5},{5,6},{6,7},{7,8},{8,9},{9,10},{10,1... | collective-permute-start | bytes 786440 | tf_op jit(solution)/shard_map/while/body/eval_jaxpr/ppermute | solution.py:13
  453.4 11.2 %collective-permute-start = (bf16[128,1024]{1,0:T(8,128)(2,1)S(1)}, bf16[128,1024]{1,0:T(8,128)(2,1)S(1)}, u32[]{:S(2)}, u32[]{:S(2)}) collective-permute-start(bf16[128,1024]{1,0:T(8,128)(2,1)S(1)} %get-tuple-element.321), channel_id=1, source_target_pairs={{0,1},{1,2},{2,3},{3,4},{4,5},{5,6},{6,7},{7,8},{8,9},{9,10},{10,1... | collective-permute-start | bytes 786440 | tf_op jit(solution)/shard_map/while/body/eval_jaxpr/ppermute | solution.py:13
  455.3 12.1 %collective-permute-start.1 = (bf16[128,1024]{1,0:T(8,128)(2,1)}, bf16[128,1024]{1,0:T(8,128)(2,1)S(1)}, u32[]{:S(2)}, u32[]{:S(2)}) collective-permute-start(bf16[128,1024]{1,0:T(8,128)(2,1)} %get-tuple-element.322), channel_id=1, source_target_pairs={{0,1},{1,2},{2,3},{3,4},{4,5},{5,6},{6,7},{7,8},{8,9},{9,10},{10,1... | collective-permute-start | bytes 786440 | tf_op jit(solution)/shard_map/while/body/eval_jaxpr/ppermute | solution.py:13
  470.2 12.4 %collective-permute-start = (bf16[128,1024]{1,0:T(8,128)(2,1)S(1)}, bf16[128,1024]{1,0:T(8,128)(2,1)S(1)}, u32[]{:S(2)}, u32[]{:S(2)}) collective-permute-start(bf16[128,1024]{1,0:T(8,128)(2,1)S(1)} %get-tuple-element.321), channel_id=1, source_target_pairs={{0,1},{1,2},{2,3},{3,4},{4,5},{5,6},{6,7},{7,8},{8,9},{9,10},{10,1... | collective-permute-start | bytes 786440 | tf_op jit(solution)/shard_map/while/body/eval_jaxpr/ppermute | solution.py:13
  472.1 13.2 %collective-permute-start.1 = (bf16[128,1024]{1,0:T(8,128)(2,1)}, bf16[128,1024]{1,0:T(8,128)(2,1)S(1)}, u32[]{:S(2)}, u32[]{:S(2)}) collective-permute-start(bf16[128,1024]{1,0:T(8,128)(2,1)} %get-tuple-element.322), channel_id=1, source_target_pairs={{0,1},{1,2},{2,3},{3,4},{4,5},{5,6},{6,7},{7,8},{8,9},{9,10},{10,1... | collective-permute-start | bytes 786440 | tf_op jit(solution)/shard_map/while/body/eval_jaxpr/ppermute | solution.py:13
  488.0 12.4 %collective-permute-start = (bf16[128,1024]{1,0:T(8,128)(2,1)S(1)}, bf16[128,1024]{1,0:T(8,128)(2,1)S(1)}, u32[]{:S(2)}, u32[]{:S(2)}) collective-permute-start(bf16[128,1024]{1,0:T(8,128)(2,1)S(1)} %get-tuple-element.321), channel_id=1, source_target_pairs={{0,1},{1,2},{2,3},{3,4},{4,5},{5,6},{6,7},{7,8},{8,9},{9,10},{10,1... | collective-permute-start | bytes 786440 | tf_op jit(solution)/shard_map/while/body/eval_jaxpr/ppermute | solution.py:13
  489.9 14.3 %collective-permute-start.1 = (bf16[128,1024]{1,0:T(8,128)(2,1)}, bf16[128,1024]{1,0:T(8,128)(2,1)S(1)}, u32[]{:S(2)}, u32[]{:S(2)}) collective-permute-start(bf16[128,1024]{1,0:T(8,128)(2,1)} %get-tuple-element.322), channel_id=1, source_target_pairs={{0,1},{1,2},{2,3},{3,4},{4,5},{5,6},{6,7},{7,8},{8,9},{9,10},{10,1... | collective-permute-start | bytes 786440 | tf_op jit(solution)/shard_map/while/body/eval_jaxpr/ppermute | solution.py:13
  507.0 12.2 %collective-permute-start = (bf16[128,1024]{1,0:T(8,128)(2,1)S(1)}, bf16[128,1024]{1,0:T(8,128)(2,1)S(1)}, u32[]{:S(2)}, u32[]{:S(2)}) collective-permute-start(bf16[128,1024]{1,0:T(8,128)(2,1)S(1)} %get-tuple-element.321), channel_id=1, source_target_pairs={{0,1},{1,2},{2,3},{3,4},{4,5},{5,6},{6,7},{7,8},{8,9},{9,10},{10,1... | collective-permute-start | bytes 786440 | tf_op jit(solution)/shard_map/while/body/eval_jaxpr/ppermute | solution.py:13
  508.9 15.4 %collective-permute-start.1 = (bf16[128,1024]{1,0:T(8,128)(2,1)}, bf16[128,1024]{1,0:T(8,128)(2,1)S(1)}, u32[]{:S(2)}, u32[]{:S(2)}) collective-permute-start(bf16[128,1024]{1,0:T(8,128)(2,1)} %get-tuple-element.322), channel_id=1, source_target_pairs={{0,1},{1,2},{2,3},{3,4},{4,5},{5,6},{6,7},{7,8},{8,9},{9,10},{10,1... | collective-permute-start | bytes 786440 | tf_op jit(solution)/shard_map/while/body/eval_jaxpr/ppermute | solution.py:13
  527.1 11.9 %collective-permute-start.3 = (bf16[128,1024]{1,0:T(8,128)(2,1)}, bf16[128,1024]{1,0:T(8,128)(2,1)S(1)}, u32[]{:S(2)}, u32[]{:S(2)}) collective-permute-start(bf16[128,1024]{1,0:T(8,128)(2,1)} %get-tuple-element.228), channel_id=1, source_target_pairs={{0,1},{1,2},{2,3},{3,4},{4,5},{5,6},{6,7},{7,8},{8,9},{9,10},{10,1... | collective-permute-start | bytes 786440 | tf_op jit(solution)/shard_map/ppermute | solution.py:13
  (1 other events, 5.8 us)
Sparse Core Ops, SparseCore 0:
  539.9 94.8 all-gather.2
